TPU v7x, 32 devices: a whole 2x2x4 slice. The times are simulated.
32 devices in a mesh: seq: 4 (over y, x), dp: 8 (over z, core).
Axes of the slice: x: 2, y: 2, z: 4, core: 2. Of those that a mesh axis runs over, the one named last changes fastest.
Arguments:
- queries: bfloat16 [8192, 1024], P(('dp', 'seq')), parts along dimension 0, may hold values from -6 to 6
- keys: bfloat16 [8192, 256], P(('dp', 'seq')), parts along dimension 0, may hold values from -6 to 6
- values: bfloat16 [8192, 256], P(('dp', 'seq')), parts along dimension 0, may hold values from -6 to 6
- out_grad: bfloat16 [8192, 1024], P(('dp', 'seq')), parts along dimension 0, may hold values from -6 to 6
- rand_blocks: int32 [128, 3], P('dp'), parts along dimension 0, may hold values from 0 to 15, as said below
- global_blocks: int32 [16], P('dp'), parts along dimension 0, may hold values from 0 to 15, as said below
Outputs:
- out: bfloat16 [8192, 1024], P(('dp', 'seq')), parts along dimension 0
- query_grad: bfloat16 [8192, 1024], P(('dp', 'seq')), parts along dimension 0
- key_grad: bfloat16 [8192, 256], P(('dp', 'seq')), parts along dimension 0
- value_grad: bfloat16 [8192, 256], P(('dp', 'seq')), parts along dimension 0
There are 8 independent parts, one for each index of `dp`. A program takes and returns all parts, laid end to end along the dimension named above; each array names one. Nothing has to cross between parts.
Inputs may be any that keep to these rules, and one draw needn't show every extreme that they name: `rand_blocks`: block j lies on index j // 4 of seq. For each index r of seq, the 12 entries of rows r * 4 to (r + 1) * 4 - 1 together with the 2 global blocks name blocks of no index more than 4 times, and blocks of some index exactly 4 times. `global_blocks`: the global blocks lie on different indices of seq.
All inputs are finite; a program needn't handle non-finite values.
Results may differ from a plain program's by a relative error of at most 0.011.
Values may be sent and summed in bfloat16 or wider, within the bound.
No kernel may reach another device: no remote copies, remote signals or barrier semaphores. Data moves between devices by JAX's collectives and lax.ppermute only.
A program may use at most 64 MiB of HBM per device.

v0:
```python
import functools

import jax
import jax.numpy as jnp
from jax import lax
from jax.experimental import pallas as pl
from jax.experimental.pallas import tpu as pltpu
from jax.sharding import PartitionSpec as P

KVH = 2
HD = 128
BLOCK = 64
GLOB = 2
RAND = 3
GROUP = 4
ENTRIES = 3 + GLOB + RAND
LOG2E = 1.4426950408889634
SCALE = HD ** (-0.5)


NN = (((1,), (0,)), ((), ()))
TN = (((0,), (0,)), ((), ()))
dot = functools.partial(lax.dot_general, preferred_element_type=jnp.float32)

KEYS = ENTRIES * BLOCK
CHUNK = 128
FACTOR = SCALE * LOG2E
ROWS = GROUP * BLOCK


def units(blocks_here):
    return [(b, h, b * KVH + h) for b in range(blocks_here) for h in range(KVH)]


def given_places(lists, blocks_here, b):
    return [lists[0][b, e] for e in range(ENTRIES)]


def dense_offsets(cycle_size, position):
    odd = position & 1
    offsets = list(range(cycle_size))
    offsets[1], offsets[2] = 1 + odd, 2 - odd
    return offsets


def dense_places(cycle_size, lists, blocks_here, b):
    rand_ref, glob_ref = lists
    me = lax.axis_index("seq").astype(jnp.int32)
    odd = lax.axis_index("dp").astype(jnp.int32) & 1

    def place(owner, local):
        offset = owner ^ me
        swapped = (odd == 1) & ((offset == 1) | (offset == 2))
        return jnp.where(swapped, 3 - offset, offset) * blocks_here + local

    def far_place(block):
        return place(lax.div(block, blocks_here), lax.rem(block, blocks_here))

    window = [b - 1, b, b + 1]
    if b == 0:
        window[0] = place(lax.rem(me + cycle_size - 1, cycle_size), blocks_here - 1)
    if b == blocks_here - 1:
        window[2] = place(lax.rem(me + 1, cycle_size), 0)
    far = [glob_ref[i] for i in range(GLOB)] + [rand_ref[i, me * blocks_here + b] for i in range(RAND)]
    return window + [far_place(block) for block in far]


def spans(table, b):
    result = []
    for e in range(ENTRIES):
        near = b + e - 1
        if e < 3 and 0 <= near < table.shape[0]:
            result.append(pl.ds(near * BLOCK, BLOCK))
        else:
            result.append(pl.ds(pl.multiple_of(table[b, e] * BLOCK, BLOCK), BLOCK))
    return result


def picked(pool, places, h):
    return jnp.concatenate([pool[place, h * HD : (h + 1) * HD] for place in places], axis=0)


def unstack(ref, b, h, value):
    for j in range(GROUP):
        c = (h * GROUP + j) * HD
        ref[b * BLOCK : (b + 1) * BLOCK, c : c + HD] = value[j * BLOCK : (j + 1) * BLOCK]


def add_terms(pool, places, h, terms):
    for e, place in enumerate(places):
        pool[place, h * HD : (h + 1) * HD] += terms[e * BLOCK : (e + 1) * BLOCK]


def gather_pool(pool, parts):
    start = 0
    for part in parts:
        pool[start : start + part.shape[0]] = part[...]
        start += part.shape[0]


def split_pool(outs, pool, factor):
    start = 0
    for out in outs:
        total = pool[start : start + out.shape[0]]
        out[...] = (total if factor is None else total * factor).astype(out.dtype)
        start += out.shape[0]


def stage_kernel(locate, count, *refs):
    sources, refs = refs[: count + 4], refs[count + 4 :]
    table, q_rows, g_rows, q_cols, g_cols, dv_pool, dk_pool, k_ref, v_ref, *refs = refs
    lists = refs[:count]
    q_ref, g_ref, sem = refs[count:]
    targets = [*lists, q_ref, g_ref, k_ref, v_ref]
    copies = [
        pltpu.make_async_copy(source, target, sem.at[i])
        for i, (source, target) in enumerate(zip(sources, targets))
    ]
    for copy in copies:
        copy.start()
    dv_pool[...] = jnp.zeros_like(dv_pool)
    dk_pool[...] = jnp.zeros_like(dk_pool)
    for copy in copies[: count + 2]:
        copy.wait()
    for b in range(table.shape[0]):
        for e, place in enumerate(locate(lists, table.shape[0], b)):
            table[b, e] = jnp.int32(place)
    for ref, rows, cols in ((q_ref, q_rows, q_cols), (g_ref, g_rows, g_cols)):
        for b, h, u in units(table.shape[0]):
            heads = [(h * GROUP + j) * HD for j in range(GROUP)]
            unit = jnp.concatenate(
                [ref[b * BLOCK : (b + 1) * BLOCK, c : c + HD] for c in heads], axis=0
            )
            rows[u * ROWS : (u + 1) * ROWS] = unit
            cols[u * HD : (u + 1) * HD] = unit.T
    for copy in copies[count + 2 :]:
        copy.wait()


def probs_kernel(count, table, q_cols, g_rows, cleared, *refs):
    parts = refs[:count][::-1]
    probs_ref, k_pool, dv_pool, *dv_refs = refs[count:]
    gather_pool(k_pool, parts)
    for b, h, u in units(table.shape[0]):
        places = spans(table, b)
        scores = dot(picked(k_pool, places, h), q_cols[u * HD : (u + 1) * HD], NN)
        chunks = [scores[i : i + CHUNK] for i in range(0, KEYS, CHUNK)]
        peaks = [jnp.max(chunk, axis=0, keepdims=True) for chunk in chunks]
        expos = [jnp.exp2((chunk - peak) * FACTOR) for chunk, peak in zip(chunks, peaks)]
        peak = functools.reduce(jnp.maximum, peaks)
        scales = [jnp.exp2((own - peak) * FACTOR) for own in peaks]
        norm = 1.0 / sum(jnp.sum(e, axis=0, keepdims=True) * r for e, r in zip(expos, scales))
        probs = [(e * (r * norm)).astype(jnp.bfloat16) for e, r in zip(expos, scales)]
        probs_b = jnp.concatenate(probs, axis=0)
        probs_ref[u * KEYS : (u + 1) * KEYS] = probs_b
        add_terms(dv_pool, places, h, dot(probs_b, g_rows[u * ROWS : (u + 1) * ROWS], NN))
    split_pool(dv_refs, dv_pool, None)


def dscores_kernel(count, table, q_rows, g_cols, probs_ref, cleared, *refs):
    parts = refs[:count][::-1]
    ds_ref, v_pool, dk_pool, *dk_refs = refs[count:]
    gather_pool(v_pool, parts)
    for b, h, u in units(table.shape[0]):
        places = spans(table, b)
        probs = probs_ref[u * KEYS : (u + 1) * KEYS].astype(jnp.float32)
        dprobs = dot(picked(v_pool, places, h), g_cols[u * HD : (u + 1) * HD], NN)
        delta = jnp.sum(probs * dprobs, axis=0, keepdims=True)
        dscores = (probs * (dprobs - delta)).astype(jnp.bfloat16)
        ds_ref[u * KEYS : (u + 1) * KEYS] = dscores
        add_terms(dk_pool, places, h, dot(dscores, q_rows[u * ROWS : (u + 1) * ROWS], NN))
    split_pool(dk_refs, dk_pool, SCALE)


def rows_kernel(table, probs_ref, ds_ref, k_pool, v_pool, out_any, qgrad_any, out_ref, qgrad_ref, sem):
    copies = []
    for b in range(table.shape[0]):
        places = spans(table, b)
        for h in range(KVH):
            span = slice((b * KVH + h) * KEYS, (b * KVH + h + 1) * KEYS)
            attended = dot(probs_ref[span], picked(v_pool, places, h), TN)
            unstack(out_ref, b, h, attended.astype(jnp.bfloat16))
            qgrad = dot(ds_ref[span], picked(k_pool, places, h), TN) * SCALE
            unstack(qgrad_ref, b, h, qgrad.astype(jnp.bfloat16))
        rows = pl.ds(b * BLOCK, BLOCK)
        for ref, target in ((out_ref, out_any), (qgrad_ref, qgrad_any)):
            copies.append(pltpu.make_async_copy(ref.at[rows], target.at[rows], sem.at[len(copies)]))
            copies[-1].start()
    for copy in copies:
        copy.wait()


SMEM = pl.BlockSpec(memory_space=pltpu.SMEM)
HBM = pl.BlockSpec(memory_space=pltpu.HBM)
VMEM = pl.BlockSpec(memory_space=pltpu.VMEM)


def run_kernel(kernel, operands, in_specs, results, scratch, products, out_spec=VMEM, aliases={}):
    flops = products * 2 * 4 * KVH * ROWS * KEYS * HD
    return pl.pallas_call(
        kernel,
        out_shape=[
            result if hasattr(result, "memory_space") else jax.ShapeDtypeStruct(*result)
            for result in results
        ],
        in_specs=in_specs + [VMEM] * (len(operands) - len(in_specs)),
        out_specs=[SMEM if hasattr(result, "memory_space") else out_spec for result in results],
        scratch_shapes=scratch,
        input_output_aliases=aliases,
        compiler_params=pltpu.CompilerParams(vmem_limit_bytes=32 * 2**20),
        cost_estimate=pl.CostEstimate(
            flops=flops, bytes_accessed=products * 2**20, transcendentals=0
        ),
    )(*operands)


def stage(locate, lists, queries, out_grad, keys, values, pool_rows):
    blocks_here = queries.shape[0] // BLOCK
    half = jnp.bfloat16
    rows = ((blocks_here * KVH * ROWS, HD), half)
    cols = ((blocks_here * KVH * HD, ROWS), half)
    narrow, wide = (keys.shape, half), (queries.shape, half)
    cleared = ((pool_rows, keys.shape[1]), jnp.float32)
    mine = (*lists, queries, out_grad, keys, values)
    return run_kernel(
        functools.partial(stage_kernel, locate, len(lists)),
        [pltpu.with_memory_space_constraint(array, pltpu.HBM) for array in mine],
        [HBM] * len(mine),
        [
            pltpu.SMEM((blocks_here, ENTRIES), jnp.int32),
            rows, rows, cols, cols, cleared, cleared, narrow, narrow,
        ],
        [
            *[pltpu.SMEM(array.shape, array.dtype) for array in lists],
            pltpu.VMEM(*wide), pltpu.VMEM(*wide),
            pltpu.SemaphoreType.DMA((len(mine),)),
        ],
        1,
    )


def attend(table, staged, key_parts, value_parts, send):
    q_rows, g_rows, q_cols, g_cols, dv_pool, dk_pool = staged
    tok_rows, width = key_parts[0].shape
    half, full = jnp.bfloat16, jnp.float32
    wide = ((tok_rows, GROUP * width), half)
    count = len(key_parts)
    pool_rows = sum(part.shape[0] for part in key_parts)
    held = ((table.shape[0] * KVH * KEYS, ROWS), half)
    sums = [(part.shape, half if i else full) for i, part in enumerate(key_parts)]
    pool, cleared = ((pool_rows, width), half), ((pool_rows, width), full)
    probs, k_pool, _, *dv = run_kernel(
        functools.partial(probs_kernel, count),
        (table, q_cols, g_rows, dv_pool, *key_parts[::-1]),
        [SMEM], [held, pool, cleared, *sums], [], 2, aliases={3: 2},
    )
    dv = send(dv, None)
    dscores, v_pool, _, *dk = run_kernel(
        functools.partial(dscores_kernel, count),
        (table, q_rows, g_cols, probs, dk_pool, *value_parts[::-1]),
        [SMEM], [held, pool, cleared, *sums], [], 2, aliases={4: 2},
    )
    dk = send(dk, dv)
    dv[1], table = lax.optimization_barrier((dv[1], table))
    out, query_grad = run_kernel(
        rows_kernel, (table, probs, dscores, k_pool, v_pool), [SMEM], [wide, wide],
        [pltpu.VMEM(*wide)] * 2 + [pltpu.SemaphoreType.DMA((2 * table.shape[0],))], 2, HBM,
    )
    dv[2:], dk[-1], query_grad = lax.optimization_barrier((dv[2:], dk[-1], query_grad))
    return out, query_grad, dk, dv


def dense_local(queries, keys, values, out_grad, rand_blocks, global_blocks):
    cycle_size = lax.axis_size("seq")
    positions = lax.axis_size("dp")

    def swap(array, part):
        pairs = []
        for position in range(positions):
            offset = dense_offsets(cycle_size, position)[part]
            pairs += [(i * positions + position, (i ^ offset) * positions + position) for i in range(cycle_size)]
        return lax.ppermute(array, ("seq", "dp"), pairs)

    def send(grads, earlier):
        sent = [grads[0]] + [None] * (cycle_size - 1)
        sent[-1] = swap(grads[-1], cycle_size - 1)
        near = grads[1:-1]
        if earlier is not None:
            near, earlier[1] = lax.optimization_barrier((near, earlier[1]))
        for part in range(1, cycle_size - 1):
            sent[part] = swap(near[part - 1], part)
        return sent

    def total(grads):
        return sum(grad.astype(jnp.float32) for grad in grads).astype(jnp.bfloat16)

    parts = range(1, cycle_size)
    key_parts = [swap(keys, part) for part in parts]
    table, *staged, keys, values = stage(
        functools.partial(dense_places, cycle_size), (rand_blocks.T, global_blocks),
        queries, out_grad, keys, values, cycle_size * keys.shape[0],
    )
    value_parts = [swap(values, part) for part in parts]
    out, query_grad, dk, dv = attend(
        table, staged, [keys, *key_parts], [values, *value_parts], send
    )
    return out, query_grad, total(dk), total(dv)


def sparse_local(queries, keys, values, out_grad, rand_blocks, global_blocks):
    cycle_size = lax.axis_size("seq")
    myself = lax.axis_index("seq").astype(jnp.int32)
    tok_rows, width = keys.shape
    blocks_here = tok_rows // BLOCK
    rand_total = RAND * blocks_here
    capacity = (rand_total + GLOB + cycle_size - 1) // cycle_size
    slot_total = cycle_size * capacity
    listed = jnp.concatenate(
        [
            rand_blocks.reshape(cycle_size, rand_total),
            jnp.broadcast_to(global_blocks[None, :], (cycle_size, GLOB)),
        ],
        axis=1,
    )
    entries = listed.shape[1]
    owners = listed // blocks_here
    local_slot = listed % blocks_here
    earlier = jnp.arange(entries)[None, :] < jnp.arange(entries)[:, None]
    same_owner = owners[:, :, None] == owners[:, None, :]
    ranking = jnp.sum(same_owner & earlier[None], axis=2)
    owners_mine = lax.dynamic_index_in_dim(owners, myself, 0, keepdims=False)
    ranking_mine = lax.dynamic_index_in_dim(ranking, myself, 0, keepdims=False)
    far_place = (blocks_here + 2 + owners_mine * capacity + ranking_mine).astype(jnp.int32)
    slot_ids = jnp.arange(slot_total)
    requester = slot_ids // capacity
    position = slot_ids % capacity
    matches = (owners[requester] == myself) & (ranking[requester] == position[:, None])
    source = jnp.sum(jnp.where(matches, local_slot[requester], 0), axis=1)

    up = [(i, (i + 1) % cycle_size) for i in range(cycle_size)]
    down = [(j, i) for i, j in up]
    pair = jnp.concatenate([keys, values], axis=1)
    before = lax.ppermute(pair[tok_rows - BLOCK :], "seq", up)
    after = lax.ppermute(pair[:BLOCK], "seq", down)
    outgoing = jnp.take(pair.reshape(blocks_here, BLOCK, 2 * width), source, axis=0)
    far = lax.all_to_all(outgoing, "seq", split_axis=0, concat_axis=0, tiled=True)
    others = [before, after, far.reshape(slot_total * BLOCK, 2 * width)]
    key_parts = [part[:, :width] for part in others]
    value_parts = [part[:, width:] for part in others]

    here = jnp.arange(blocks_here, dtype=jnp.int32)[:, None]
    ahead = jnp.where(here == 0, blocks_here, here - 1)
    behind = jnp.where(here == blocks_here - 1, blocks_here + 1, here + 1)
    table = jnp.concatenate(
        [
            ahead,
            here,
            behind,
            jnp.broadcast_to(far_place[None, rand_total:], (blocks_here, GLOB)),
            far_place[:rand_total].reshape(blocks_here, RAND),
        ],
        axis=1,
    )
    landing = (source[:, None] == jnp.arange(blocks_here)[None, :]).astype(jnp.bfloat16)

    def send(grads, earlier):
        own, grad_before, grad_after, grad_far = grads
        last_rim = lax.ppermute(grad_before, "seq", down)
        first_rim = lax.ppermute(grad_after, "seq", up)
        returned = lax.all_to_all(
            grad_far.reshape(slot_total, BLOCK, width),
            "seq", split_axis=0, concat_axis=0, tiled=True,
        )
        return [own, last_rim, first_rim, returned]

    def total(grads):
        own, last_rim, first_rim, returned = grads
        landed = jnp.einsum("sq,sbx->qbx", landing, returned, preferred_element_type=jnp.float32)
        sums = own.reshape(blocks_here, BLOCK, width) + landed
        sums = sums.at[blocks_here - 1].add(last_rim.astype(jnp.float32))
        sums = sums.at[0].add(first_rim.astype(jnp.float32))
        return sums.reshape(tok_rows, width).astype(jnp.bfloat16)

    pool_rows = tok_rows + sum(part.shape[0] for part in key_parts)
    table, *staged, keys, values = stage(
        given_places, (table,), queries, out_grad, keys, values, pool_rows
    )
    out, query_grad, dk, dv = attend(
        table, staged, [keys, *key_parts], [values, *value_parts], send
    )
    return out, query_grad, total(dk), total(dv)


def local(queries, keys, values, out_grad, rand_blocks, global_blocks):
    cycle_size = lax.axis_size("seq")
    blocks_here = queries.shape[0] // BLOCK
    capacity = (RAND * blocks_here + GLOB + cycle_size - 1) // cycle_size
    dense = capacity >= blocks_here and cycle_size == 4
    plan = dense_local if dense else sparse_local
    return plan(queries, keys, values, out_grad, rand_blocks, global_blocks)


def solution(mesh):
    rows = P(("dp", "seq"), None)
    return jax.shard_map(
        local,
        mesh=mesh,
        in_specs=(rows, rows, rows, rows, P("dp", None), P("dp")),
        out_specs=(rows, rows, rows, rows),
        check_vma=False,
    )
```

profile of v0, /device:TPU:0, one launch (start us, length us, event | category | flops | bytes accessed | tf_op | source)
XLA Modules:
  0.0 29.6 jit_solution(18427973713366988137)
XLA Ops:
  0.6 4.0 %collective-permute-start = (bf16[256,256]{1,0:T(8,128)(2,1)}, bf16[256,256]{1,0:T(8,128)(2,1)S(1)}, u32[]{:S(2)}, u32[]{:S(2)}) collective-permute-start(bf16[256,256]{1,0:T(8,128)(2,1)} %refs_4_.1), channel_id=1, source_target_pairs={{0,24},{8,16},{16,8},{24,0},{1,25},{9,17},{17,9},{25,1},{2,26},{10... | collective-permute-start | bytes 393224 | tf_op jit(solution)/shard_map/ppermute | solution.py:282
  4.6 0.5 %collective-permute-start.2 = (bf16[256,256]{1,0:T(8,128)(2,1)}, bf16[256,256]{1,0:T(8,128)(2,1)S(1)}, u32[]{:S(2)}, u32[]{:S(2)}) collective-permute-start(bf16[256,256]{1,0:T(8,128)(2,1)} %refs_4_.1), channel_id=1, source_target_pairs={{0,8},{8,0},{16,24},{24,16},{1,17},{9,25},{17,1},{25,9},{2,10},{10... | collective-permute-start | bytes 393224 | tf_op jit(solution)/shard_map/ppermute | solution.py:282
  5.1 0.1 collective-permute-start.1
  5.2 1.7 %shard_map.93 = (s32[4,8]{1,0:T(4,128)S(4)}, bf16[2048,128]{1,0:T(8,128)(2,1)S(1)}, bf16[2048,128]{1,0:T(8,128)(2,1)S(1)}, bf16[1024,256]{1,0:T(8,128)(2,1)S(1)}...) custom-call(s32[3,16]{1,0:T(4,128)} %bitcast.1, ...), custom_call_target="tpu_custom_call" | custom-call | flops 268435456 | bytes 1048576 | tf_op jit(solution)/shard_map/pallas_call | solution.py:200
  7.0 2.0 %collective-permute-start.5 = (bf16[256,256]{1,0:T(8,128)(2,1)S(1)}, bf16[256,256]{1,0:T(8,128)(2,1)S(1)}, u32[]{:S(2)}, u32[]{:S(2)}) collective-permute-start(bf16[256,256]{1,0:T(8,128)(2,1)S(1)} %get-tuple-element.45.refs_3_), channel_id=1, source_target_pairs={{0,8},{8,0},{16,24},{24,16},{1,17},{9,25},{17,1},{25,9},{2,10},{10... | collective-permute-start | bytes 393224 | tf_op jit(solution)/shard_map/ppermute | solution.py:282
  8.9 1.5 %collective-permute-start.4 = (bf16[256,256]{1,0:T(8,128)(2,1)S(1)}, bf16[256,256]{1,0:T(8,128)(2,1)S(1)}, u32[]{:S(2)}, u32[]{:S(2)}) collective-permute-start(bf16[256,256]{1,0:T(8,128)(2,1)S(1)} %get-tuple-element.45.refs_3_), channel_id=1, source_target_pairs={{0,16},{8,24},{16,0},{24,8},{1,9},{9,1},{17,25},{25,17},{2,18},{10... | collective-permute-start | bytes 393224 | tf_op jit(solution)/shard_map/ppermute | solution.py:282
  10.4 0.0 collective-permute-done.refs_0_
  10.4 1.6 %collective-permute-start.3 = (bf16[256,256]{1,0:T(8,128)(2,1)S(1)}, bf16[256,256]{1,0:T(8,128)(2,1)S(1)}, u32[]{:S(2)}, u32[]{:S(2)}) collective-permute-start(bf16[256,256]{1,0:T(8,128)(2,1)S(1)} %get-tuple-element.45.refs_3_), channel_id=1, source_target_pairs={{0,24},{8,16},{16,8},{24,0},{1,25},{9,17},{17,9},{25,1},{2,26},{10... | collective-permute-start | bytes 393224 | tf_op jit(solution)/shard_map/ppermute | solution.py:282
  12.1 0.3 collective-permute-done.2.refs_2_
  12.4 0.0 collective-permute-done.1.refs_1_
  12.4 1.8 %shard_map.94 = (bf16[4096,256]{1,0:T(8,128)(2,1)S(1)}, bf16[1024,256]{1,0:T(8,128)(2,1)S(1)}, f32[1024,256]{1,0:T(8,128)S(1)}, f32[256,256]{1,0:T(8,128)S(1)}, ...) custom-call(s32[4,8]{1,0:T(4,128)S(4)} %get-tuple-element.50.table, ...), custom_call_target="tpu_custom_call", output_to_operand_aliasing={{2}: (3, {})} | custom-call | flops 536870912 | bytes 2097152 | tf_op jit(solution)/shard_map/pallas_call | solution.py:200
  14.2 1.7 %collective-permute-start.6 = (bf16[256,256]{1,0:T(8,128)(2,1)S(1)}, bf16[256,256]{1,0:T(8,128)(2,1)S(1)}, u32[]{:S(2)}, u32[]{:S(2)}) collective-permute-start(bf16[256,256]{1,0:T(8,128)(2,1)S(1)} %get-tuple-element.48), channel_id=1, source_target_pairs={{0,8},{8,0},{16,24},{24,16},{1,17},{9,25},{17,1},{25,9},{2,10},{10... | collective-permute-start | bytes 393224 | tf_op jit(solution)/shard_map/ppermute | solution.py:282
  15.9 0.6 %collective-permute-start.7 = (bf16[256,256]{1,0:T(8,128)(2,1)S(1)}, bf16[256,256]{1,0:T(8,128)(2,1)S(1)}, u32[]{:S(2)}, u32[]{:S(2)}) collective-permute-start(bf16[256,256]{1,0:T(8,128)(2,1)S(1)} %get-tuple-element.55), channel_id=1, source_target_pairs={{0,16},{8,24},{16,0},{24,8},{1,9},{9,1},{17,25},{25,17},{2,18},{10... | collective-permute-start | bytes 393224 | tf_op jit(solution)/shard_map/ppermute | solution.py:282
  16.6 0.0 collective-permute-done.5.refs_2_
  16.6 1.2 %collective-permute-start.8 = (bf16[256,256]{1,0:T(8,128)(2,1)S(1)}, bf16[256,256]{1,0:T(8,128)(2,1)S(1)}, u32[]{:S(2)}, u32[]{:S(2)}) collective-permute-start(bf16[256,256]{1,0:T(8,128)(2,1)S(1)} %get-tuple-element.56), channel_id=1, source_target_pairs={{0,24},{8,16},{16,8},{24,0},{1,25},{9,17},{17,9},{25,1},{2,26},{10... | collective-permute-start | bytes 393224 | tf_op jit(solution)/shard_map/ppermute | solution.py:282
  17.8 0.0 collective-permute-done.4.refs_1_
  17.8 0.0 collective-permute-done.3.refs_0_
  17.8 2.0 %shard_map.95 = (bf16[4096,256]{1,0:T(8,128)(2,1)S(1)}, bf16[1024,256]{1,0:T(8,128)(2,1)S(1)}, f32[1024,256]{1,0:T(8,128)S(1)}, f32[256,256]{1,0:T(8,128)S(1)}, ...) custom-call(s32[4,8]{1,0:T(4,128)S(4)} %get-tuple-element.50.table, ...), custom_call_target="tpu_custom_call", output_to_operand_aliasing={{2}: (4, {})} | custom-call | flops 536870912 | bytes 2097152 | tf_op jit(solution)/shard_map/pallas_call | solution.py:200
  19.9 2.8 %collective-permute-start.9 = (bf16[256,256]{1,0:T(8,128)(2,1)S(1)}, bf16[256,256]{1,0:T(8,128)(2,1)S(1)}, u32[]{:S(2)}, u32[]{:S(2)}) collective-permute-start(bf16[256,256]{1,0:T(8,128)(2,1)S(1)} %get-tuple-element.57), channel_id=1, source_target_pairs={{0,24},{8,16},{16,8},{24,0},{1,25},{9,17},{17,9},{25,1},{2,26},{10... | collective-permute-start | bytes 393224 | tf_op jit(solution)/shard_map/ppermute | solution.py:282
  22.6 0.0 collective-permute-done.6
  22.6 0.0 collective-permute-start.10
  22.6 0.8 %collective-permute-start.11 = (bf16[256,256]{1,0:T(8,128)(2,1)S(1)}, bf16[256,256]{1,0:T(8,128)(2,1)S(1)}, u32[]{:S(2)}, u32[]{:S(2)}) collective-permute-start(bf16[256,256]{1,0:T(8,128)(2,1)S(1)} %get-tuple-element.62), channel_id=1, source_target_pairs={{0,16},{8,24},{16,0},{24,8},{1,9},{9,1},{17,25},{25,17},{2,18},{10... | collective-permute-start | bytes 393224 | tf_op jit(solution)/shard_map/ppermute | solution.py:282
  23.4 2.0 %shard_map.96 = (bf16[256,1024]{1,0:T(8,128)(2,1)}, bf16[256,1024]{1,0:T(8,128)(2,1)}) custom-call(s32[4,8]{1,0:T(4,128)S(4)} %get-tuple-element.50.table, bf16[4096,256]{1,0:T(8,128)(2,1)S(1)} %get-tuple-element.43.probs_ref, bf16[4096,256]{1,0:T(8,128)(2,1)S(1)} %get-tuple-element.51.ds_ref, bf16[1024,256]{1,0:T(8,128)(2,1)S(1)} %get-tuple-element.52.k_pool, ...), custom_call_target="tpu_custom_call" | custom-call | flops 536870912 | bytes 2097152 | tf_op jit(solution)/shard_map/pallas_call | solution.py:200
  25.5 1.0 %collective-permute-done.7 = bf16[256,256]{1,0:T(8,128)(2,1)S(1)} collective-permute-done((bf16[256,256]{1,0:T(8,128)(2,1)S(1)}, bf16[256,256]{1,0:T(8,128)(2,1)S(1)}, u32[]{:S(2)}, u32[]{:S(2)}) %collective-permute-start.7) | collective-permute-done | bytes 131104 | tf_op jit(solution)/shard_map/ppermute | solution.py:282
  26.4 0.0 collective-permute-done.8
  26.4 0.4 %collective-permute-done.9 = bf16[256,256]{1,0:T(8,128)(2,1)S(1)} collective-permute-done((bf16[256,256]{1,0:T(8,128)(2,1)S(1)}, bf16[256,256]{1,0:T(8,128)(2,1)S(1)}, u32[]{:S(2)}, u32[]{:S(2)}) %collective-permute-start.9) | collective-permute-done | bytes 131104 | tf_op jit(solution)/shard_map/ppermute | solution.py:282
  26.9 0.7 %add_convert_fusion = bf16[256,256]{1,0:T(8,128)(2,1)} fusion(bf16[256,256]{1,0:T(8,128)(2,1)S(1)} %collective-permute-done.8, bf16[256,256]{1,0:T(8,128)(2,1)S(1)} %collective-permute-done.7, f32[256,256]{1,0:T(8,128)S(1)} %get-tuple-element.64, bf16[256,256]{1,0:T(8,128)(2,1)S(1)} %collective-permute-done.6), kind=kLoop, calls=%fused_computation | loop fusion | flops 458752 | bytes 786432 | tf_op jit(solution)/shard_map/convert_element_type | solution.py:295
  27.6 0.8 %collective-permute-done.10 = bf16[256,256]{1,0:T(8,128)(2,1)S(1)} collective-permute-done((bf16[256,256]{1,0:T(8,128)(2,1)S(1)}, bf16[256,256]{1,0:T(8,128)(2,1)S(1)}, u32[]{:S(2)}, u32[]{:S(2)}) %collective-permute-start.10) | collective-permute-done | bytes 131104 | tf_op jit(solution)/shard_map/ppermute | solution.py:282
  28.4 0.6 %collective-permute-done.11 = bf16[256,256]{1,0:T(8,128)(2,1)S(1)} collective-permute-done((bf16[256,256]{1,0:T(8,128)(2,1)S(1)}, bf16[256,256]{1,0:T(8,128)(2,1)S(1)}, u32[]{:S(2)}, u32[]{:S(2)}) %collective-permute-start.11) | collective-permute-done | bytes 131104 | tf_op jit(solution)/shard_map/ppermute | solution.py:282
  28.9 0.7 %add_convert_fusion.1 = bf16[256,256]{1,0:T(8,128)(2,1)} fusion(bf16[256,256]{1,0:T(8,128)(2,1)S(1)} %collective-permute-done.9, bf16[256,256]{1,0:T(8,128)(2,1)S(1)} %collective-permute-done.11, f32[256,256]{1,0:T(8,128)S(1)} %get-tuple-element.60, bf16[256,256]{1,0:T(8,128)(2,1)S(1)} %collective-permute-done.10), kind=kLoop, calls=%fused_computation.1 | loop fusion | flops 458752 | bytes 786432 | tf_op jit(solution)/shard_map/convert_element_type | solution.py:295
Async XLA Ops:
  0.6 9.8 %collective-permute-start = (bf16[256,256]{1,0:T(8,128)(2,1)}, bf16[256,256]{1,0:T(8,128)(2,1)S(1)}, u32[]{:S(2)}, u32[]{:S(2)}) collective-permute-start(bf16[256,256]{1,0:T(8,128)(2,1)} %refs_4_.1), channel_id=1, source_target_pairs={{0,24},{8,16},{16,8},{24,0},{1,25},{9,17},{17,9},{25,1},{2,26},{10... | collective-permute-start | bytes 393224 | tf_op jit(solution)/shard_map/ppermute | solution.py:282
  4.6 7.8 %collective-permute-start.2 = (bf16[256,256]{1,0:T(8,128)(2,1)}, bf16[256,256]{1,0:T(8,128)(2,1)S(1)}, u32[]{:S(2)}, u32[]{:S(2)}) collective-permute-start(bf16[256,256]{1,0:T(8,128)(2,1)} %refs_4_.1), channel_id=1, source_target_pairs={{0,8},{8,0},{16,24},{24,16},{1,17},{9,25},{17,1},{25,9},{2,10},{10... | collective-permute-start | bytes 393224 | tf_op jit(solution)/shard_map/ppermute | solution.py:282
  5.1 7.3 %collective-permute-start.1 = (bf16[256,256]{1,0:T(8,128)(2,1)}, bf16[256,256]{1,0:T(8,128)(2,1)S(1)}, u32[]{:S(2)}, u32[]{:S(2)}) collective-permute-start(bf16[256,256]{1,0:T(8,128)(2,1)} %refs_4_.1), channel_id=1, source_target_pairs={{0,16},{8,24},{16,0},{24,8},{1,9},{9,1},{17,25},{25,17},{2,18},{10... | collective-permute-start | bytes 393224 | tf_op jit(solution)/shard_map/ppermute | solution.py:282
  7.0 9.6 %collective-permute-start.5 = (bf16[256,256]{1,0:T(8,128)(2,1)S(1)}, bf16[256,256]{1,0:T(8,128)(2,1)S(1)}, u32[]{:S(2)}, u32[]{:S(2)}) collective-permute-start(bf16[256,256]{1,0:T(8,128)(2,1)S(1)} %get-tuple-element.45.refs_3_), channel_id=1, source_target_pairs={{0,8},{8,0},{16,24},{24,16},{1,17},{9,25},{17,1},{25,9},{2,10},{10... | collective-permute-start | bytes 393224 | tf_op jit(solution)/shard_map/ppermute | solution.py:282
  8.9 8.9 %collective-permute-start.4 = (bf16[256,256]{1,0:T(8,128)(2,1)S(1)}, bf16[256,256]{1,0:T(8,128)(2,1)S(1)}, u32[]{:S(2)}, u32[]{:S(2)}) collective-permute-start(bf16[256,256]{1,0:T(8,128)(2,1)S(1)} %get-tuple-element.45.refs_3_), channel_id=1, source_target_pairs={{0,16},{8,24},{16,0},{24,8},{1,9},{9,1},{17,25},{25,17},{2,18},{10... | collective-permute-start | bytes 393224 | tf_op jit(solution)/shard_map/ppermute | solution.py:282
  10.4 7.4 %collective-permute-start.3 = (bf16[256,256]{1,0:T(8,128)(2,1)S(1)}, bf16[256,256]{1,0:T(8,128)(2,1)S(1)}, u32[]{:S(2)}, u32[]{:S(2)}) collective-permute-start(bf16[256,256]{1,0:T(8,128)(2,1)S(1)} %get-tuple-element.45.refs_3_), channel_id=1, source_target_pairs={{0,24},{8,16},{16,8},{24,0},{1,25},{9,17},{17,9},{25,1},{2,26},{10... | collective-permute-start | bytes 393224 | tf_op jit(solution)/shard_map/ppermute | solution.py:282
  14.2 8.4 %collective-permute-start.6 = (bf16[256,256]{1,0:T(8,128)(2,1)S(1)}, bf16[256,256]{1,0:T(8,128)(2,1)S(1)}, u32[]{:S(2)}, u32[]{:S(2)}) collective-permute-start(bf16[256,256]{1,0:T(8,128)(2,1)S(1)} %get-tuple-element.48), channel_id=1, source_target_pairs={{0,8},{8,0},{16,24},{24,16},{1,17},{9,25},{17,1},{25,9},{2,10},{10... | collective-permute-start | bytes 393224 | tf_op jit(solution)/shard_map/ppermute | solution.py:282
  15.9 10.5 %collective-permute-start.7 = (bf16[256,256]{1,0:T(8,128)(2,1)S(1)}, bf16[256,256]{1,0:T(8,128)(2,1)S(1)}, u32[]{:S(2)}, u32[]{:S(2)}) collective-permute-start(bf16[256,256]{1,0:T(8,128)(2,1)S(1)} %get-tuple-element.55), channel_id=1, source_target_pairs={{0,16},{8,24},{16,0},{24,8},{1,9},{9,1},{17,25},{25,17},{2,18},{10... | collective-permute-start | bytes 393224 | tf_op jit(solution)/shard_map/ppermute | solution.py:282
  16.6 9.9 %collective-permute-start.8 = (bf16[256,256]{1,0:T(8,128)(2,1)S(1)}, bf16[256,256]{1,0:T(8,128)(2,1)S(1)}, u32[]{:S(2)}, u32[]{:S(2)}) collective-permute-start(bf16[256,256]{1,0:T(8,128)(2,1)S(1)} %get-tuple-element.56), channel_id=1, source_target_pairs={{0,24},{8,16},{16,8},{24,0},{1,25},{9,17},{17,9},{25,1},{2,26},{10... | collective-permute-start | bytes 393224 | tf_op jit(solution)/shard_map/ppermute | solution.py:282
  19.9 7.0 %collective-permute-start.9 = (bf16[256,256]{1,0:T(8,128)(2,1)S(1)}, bf16[256,256]{1,0:T(8,128)(2,1)S(1)}, u32[]{:S(2)}, u32[]{:S(2)}) collective-permute-start(bf16[256,256]{1,0:T(8,128)(2,1)S(1)} %get-tuple-element.57), channel_id=1, source_target_pairs={{0,24},{8,16},{16,8},{24,0},{1,25},{9,17},{17,9},{25,1},{2,26},{10... | collective-permute-start | bytes 393224 | tf_op jit(solution)/shard_map/ppermute | solution.py:282
  22.6 5.7 %collective-permute-start.10 = (bf16[256,256]{1,0:T(8,128)(2,1)S(1)}, bf16[256,256]{1,0:T(8,128)(2,1)S(1)}, u32[]{:S(2)}, u32[]{:S(2)}) collective-permute-start(bf16[256,256]{1,0:T(8,128)(2,1)S(1)} %get-tuple-element.61), channel_id=1, source_target_pairs={{0,8},{8,0},{16,24},{24,16},{1,17},{9,25},{17,1},{25,9},{2,10},{10... | collective-permute-start | bytes 393224 | tf_op jit(solution)/shard_map/ppermute | solution.py:282
  22.6 6.3 %collective-permute-start.11 = (bf16[256,256]{1,0:T(8,128)(2,1)S(1)}, bf16[256,256]{1,0:T(8,128)(2,1)S(1)}, u32[]{:S(2)}, u32[]{:S(2)}) collective-permute-start(bf16[256,256]{1,0:T(8,128)(2,1)S(1)} %get-tuple-element.62), channel_id=1, source_target_pairs={{0,16},{8,24},{16,0},{24,8},{1,9},{9,1},{17,25},{25,17},{2,18},{10... | collective-permute-start | bytes 393224 | tf_op jit(solution)/shard_map/ppermute | solution.py:282
where the time goes:
time: 29.8 us; the launch traced here: 29.6 us
  starting transfers between devices  16.8 us (56%)
  Pallas kernels  7.65 us (26%)
  waiting for transfers between devices  3.06 us (10%)
  other arithmetic  1.43 us (5%)
  between operations  0.68 us (2%)
    ppermute x12, starting transfers between devices, swap(): return lax.ppermute(array, ('seq', 'dp'), pairs)  16.8 us
    pallas_call x4, Pallas kernels, run_kernel(): pl.pallas_call(kernel, out_shape=[result if hasattr(result, 'memory_space...  7.65 us
    ppermute x12, waiting for transfers between devices, swap(): return lax.ppermute(array, ('seq', 'dp'), pairs)  3.06 us
    convert_element_type x2, other arithmetic, total(): sum((grad.astype(jnp.float32) for grad in grads)).astype(jnp.bfloat16)  1.43 us
  transfers between devices with their start and end apart: 12, of which 5 were waited for; matrix products, arithmetic and copies ran while one was open for 2% of the time, Pallas kernels for 26%

commit v1 on v0

--- a/solution.py
+++ b/solution.py
@@ -138,7 +138,7 @@
 
 
 def probs_kernel(count, table, q_cols, g_rows, cleared, *refs):
-    parts = refs[:count][::-1]
+    parts = [*refs[: count - 2], refs[count - 1], refs[count - 2]]
     probs_ref, k_pool, dv_pool, *dv_refs = refs[count:]
     gather_pool(k_pool, parts)
     for b, h, u in units(table.shape[0]):
@@ -251,7 +251,7 @@
     pool, cleared = ((pool_rows, width), half), ((pool_rows, width), full)
     probs, k_pool, _, *dv = run_kernel(
         functools.partial(probs_kernel, count),
-        (table, q_cols, g_rows, dv_pool, *key_parts[::-1]),
+        (table, q_cols, g_rows, dv_pool, *key_parts[:-2], *key_parts[:-3:-1]),
         [SMEM], [held, pool, cleared, *sums], [], 2, aliases={3: 2},
     )
     dv = send(dv, None)

time: 29.8 us -> 30.1 us (1.010)
  waiting for transfers between devices: 3.06 us -> 4.33 us
  starting transfers between devices: 16.8 us -> 15.9 us
    ppermute x12, waiting for transfers between devices: 3.06 us -> 4.33 us  [swap(): return lax.ppermute(array, ('seq', 'dp'), pairs)]
    ppermute x12, starting transfers between devices: 16.8 us -> 15.9 us  [swap(): return lax.ppermute(array, ('seq', 'dp'), pairs)]
where the time goes in v1:
time: 30.1 us; the launch traced here: 30 us
  starting transfers between devices  15.9 us (53%)
  Pallas kernels  7.65 us (25%)
  waiting for transfers between devices  4.33 us (14%)
  other arithmetic  1.43 us (5%)
  between operations  0.68 us (2%)
    ppermute x12, starting transfers between devices, swap(): return lax.ppermute(array, ('seq', 'dp'), pairs)  15.9 us
    pallas_call x4, Pallas kernels, run_kernel(): pl.pallas_call(kernel, out_shape=[result if hasattr(result, 'memory_space...  7.65 us
    ppermute x12, waiting for transfers between devices, swap(): return lax.ppermute(array, ('seq', 'dp'), pairs)  4.33 us
    convert_element_type x2, other arithmetic, total(): sum((grad.astype(jnp.float32) for grad in grads)).astype(jnp.bfloat16)  1.43 us
  transfers between devices with their start and end apart: 12, of which 5 were waited for; matrix products, arithmetic and copies ran while one was open for 2% of the time, Pallas kernels for 26%

profile of v1, /device:TPU:0, one launch (start us, length us, event | category | flops | bytes accessed | tf_op | source)
XLA Modules:
  0.0 30.0 jit_solution(5035288866827386771)
XLA Ops:
  0.6 3.0 %collective-permute-start = (bf16[256,256]{1,0:T(8,128)(2,1)}, bf16[256,256]{1,0:T(8,128)(2,1)S(1)}, u32[]{:S(2)}, u32[]{:S(2)}) collective-permute-start(bf16[256,256]{1,0:T(8,128)(2,1)} %refs_4_.1), channel_id=1, source_target_pairs={{0,8},{8,0},{16,24},{24,16},{1,17},{9,25},{17,1},{25,9},{2,10},{10... | collective-permute-start | bytes 393224 | tf_op jit(solution)/shard_map/ppermute | solution.py:282
  3.6 1.5 %collective-permute-start.2 = (bf16[256,256]{1,0:T(8,128)(2,1)}, bf16[256,256]{1,0:T(8,128)(2,1)S(1)}, u32[]{:S(2)}, u32[]{:S(2)}) collective-permute-start(bf16[256,256]{1,0:T(8,128)(2,1)} %refs_4_.1), channel_id=1, source_target_pairs={{0,16},{8,24},{16,0},{24,8},{1,9},{9,1},{17,25},{25,17},{2,18},{10... | collective-permute-start | bytes 393224 | tf_op jit(solution)/shard_map/ppermute | solution.py:282
  5.2 0.0 collective-permute-start.1
  5.2 1.7 %shard_map.93 = (s32[4,8]{1,0:T(4,128)S(4)}, bf16[2048,128]{1,0:T(8,128)(2,1)S(1)}, bf16[2048,128]{1,0:T(8,128)(2,1)S(1)}, bf16[1024,256]{1,0:T(8,128)(2,1)S(1)}...) custom-call(s32[3,16]{1,0:T(4,128)} %bitcast.1, ...), custom_call_target="tpu_custom_call" | custom-call | flops 268435456 | bytes 1048576 | tf_op jit(solution)/shard_map/pallas_call | solution.py:200
  6.9 2.0 %collective-permute-start.5 = (bf16[256,256]{1,0:T(8,128)(2,1)S(1)}, bf16[256,256]{1,0:T(8,128)(2,1)S(1)}, u32[]{:S(2)}, u32[]{:S(2)}) collective-permute-start(bf16[256,256]{1,0:T(8,128)(2,1)S(1)} %get-tuple-element.45.refs_3_), channel_id=1, source_target_pairs={{0,8},{8,0},{16,24},{24,16},{1,17},{9,25},{17,1},{25,9},{2,10},{10... | collective-permute-start | bytes 393224 | tf_op jit(solution)/shard_map/ppermute | solution.py:282
  8.9 1.5 %collective-permute-start.4 = (bf16[256,256]{1,0:T(8,128)(2,1)S(1)}, bf16[256,256]{1,0:T(8,128)(2,1)S(1)}, u32[]{:S(2)}, u32[]{:S(2)}) collective-permute-start(bf16[256,256]{1,0:T(8,128)(2,1)S(1)} %get-tuple-element.45.refs_3_), channel_id=1, source_target_pairs={{0,16},{8,24},{16,0},{24,8},{1,9},{9,1},{17,25},{25,17},{2,18},{10... | collective-permute-start | bytes 393224 | tf_op jit(solution)/shard_map/ppermute | solution.py:282
  10.4 0.0 collective-permute-done.refs_1_
  10.4 0.7 %collective-permute-start.3 = (bf16[256,256]{1,0:T(8,128)(2,1)S(1)}, bf16[256,256]{1,0:T(8,128)(2,1)S(1)}, u32[]{:S(2)}, u32[]{:S(2)}) collective-permute-start(bf16[256,256]{1,0:T(8,128)(2,1)S(1)} %get-tuple-element.45.refs_3_), channel_id=1, source_target_pairs={{0,24},{8,16},{16,8},{24,0},{1,25},{9,17},{17,9},{25,1},{2,26},{10... | collective-permute-start | bytes 393224 | tf_op jit(solution)/shard_map/ppermute | solution.py:282
  11.2 0.0 collective-permute-done.2.refs_3_
  11.2 1.6 %collective-permute-done.1.refs_2_ = bf16[256,256]{1,0:T(8,128)(2,1)S(1)} collective-permute-done((bf16[256,256]{1,0:T(8,128)(2,1)}, bf16[256,256]{1,0:T(8,128)(2,1)S(1)}, u32[]{:S(2)}, u32[]{:S(2)}) %collective-permute-start.1) | collective-permute-done | bytes 131104 | tf_op jit(solution)/shard_map/ppermute | solution.py:282
  12.7 1.8 %shard_map.94 = (bf16[4096,256]{1,0:T(8,128)(2,1)S(1)}, bf16[1024,256]{1,0:T(8,128)(2,1)S(1)}, f32[1024,256]{1,0:T(8,128)S(1)}, f32[256,256]{1,0:T(8,128)S(1)}, ...) custom-call(s32[4,8]{1,0:T(4,128)S(4)} %get-tuple-element.50.table, ...), custom_call_target="tpu_custom_call", output_to_operand_aliasing={{2}: (3, {})} | custom-call | flops 536870912 | bytes 2097152 | tf_op jit(solution)/shard_map/pallas_call | solution.py:200
  14.6 1.3 %collective-permute-start.6 = (bf16[256,256]{1,0:T(8,128)(2,1)S(1)}, bf16[256,256]{1,0:T(8,128)(2,1)S(1)}, u32[]{:S(2)}, u32[]{:S(2)}) collective-permute-start(bf16[256,256]{1,0:T(8,128)(2,1)S(1)} %get-tuple-element.48), channel_id=1, source_target_pairs={{0,8},{8,0},{16,24},{24,16},{1,17},{9,25},{17,1},{25,9},{2,10},{10... | collective-permute-start | bytes 393224 | tf_op jit(solution)/shard_map/ppermute | solution.py:282
  15.9 0.5 %collective-permute-start.7 = (bf16[256,256]{1,0:T(8,128)(2,1)S(1)}, bf16[256,256]{1,0:T(8,128)(2,1)S(1)}, u32[]{:S(2)}, u32[]{:S(2)}) collective-permute-start(bf16[256,256]{1,0:T(8,128)(2,1)S(1)} %get-tuple-element.55), channel_id=1, source_target_pairs={{0,16},{8,24},{16,0},{24,8},{1,9},{9,1},{17,25},{25,17},{2,18},{10... | collective-permute-start | bytes 393224 | tf_op jit(solution)/shard_map/ppermute | solution.py:282
  16.4 0.0 collective-permute-done.5.refs_2_
  16.4 1.8 %collective-permute-start.8 = (bf16[256,256]{1,0:T(8,128)(2,1)S(1)}, bf16[256,256]{1,0:T(8,128)(2,1)S(1)}, u32[]{:S(2)}, u32[]{:S(2)}) collective-permute-start(bf16[256,256]{1,0:T(8,128)(2,1)S(1)} %get-tuple-element.56), channel_id=1, source_target_pairs={{0,24},{8,16},{16,8},{24,0},{1,25},{9,17},{17,9},{25,1},{2,26},{10... | collective-permute-start | bytes 393224 | tf_op jit(solution)/shard_map/ppermute | solution.py:282
  18.2 0.0 collective-permute-done.4.refs_1_
  18.2 0.0 collective-permute-done.3.refs_0_
  18.2 2.0 %shard_map.95 = (bf16[4096,256]{1,0:T(8,128)(2,1)S(1)}, bf16[1024,256]{1,0:T(8,128)(2,1)S(1)}, f32[1024,256]{1,0:T(8,128)S(1)}, f32[256,256]{1,0:T(8,128)S(1)}, ...) custom-call(s32[4,8]{1,0:T(4,128)S(4)} %get-tuple-element.50.table, ...), custom_call_target="tpu_custom_call", output_to_operand_aliasing={{2}: (4, {})} | custom-call | flops 536870912 | bytes 2097152 | tf_op jit(solution)/shard_map/pallas_call | solution.py:200
  20.2 1.5 %collective-permute-start.9 = (bf16[256,256]{1,0:T(8,128)(2,1)S(1)}, bf16[256,256]{1,0:T(8,128)(2,1)S(1)}, u32[]{:S(2)}, u32[]{:S(2)}) collective-permute-start(bf16[256,256]{1,0:T(8,128)(2,1)S(1)} %get-tuple-element.57), channel_id=1, source_target_pairs={{0,24},{8,16},{16,8},{24,0},{1,25},{9,17},{17,9},{25,1},{2,26},{10... | collective-permute-start | bytes 393224 | tf_op jit(solution)/shard_map/ppermute | solution.py:282
  21.7 0.0 collective-permute-done.6
  21.7 1.1 %collective-permute-start.10 = (bf16[256,256]{1,0:T(8,128)(2,1)S(1)}, bf16[256,256]{1,0:T(8,128)(2,1)S(1)}, u32[]{:S(2)}, u32[]{:S(2)}) collective-permute-start(bf16[256,256]{1,0:T(8,128)(2,1)S(1)} %get-tuple-element.61), channel_id=1, source_target_pairs={{0,8},{8,0},{16,24},{24,16},{1,17},{9,25},{17,1},{25,9},{2,10},{10... | collective-permute-start | bytes 393224 | tf_op jit(solution)/shard_map/ppermute | solution.py:282
  22.8 1.0 %collective-permute-start.11 = (bf16[256,256]{1,0:T(8,128)(2,1)S(1)}, bf16[256,256]{1,0:T(8,128)(2,1)S(1)}, u32[]{:S(2)}, u32[]{:S(2)}) collective-permute-start(bf16[256,256]{1,0:T(8,128)(2,1)S(1)} %get-tuple-element.62), channel_id=1, source_target_pairs={{0,16},{8,24},{16,0},{24,8},{1,9},{9,1},{17,25},{25,17},{2,18},{10... | collective-permute-start | bytes 393224 | tf_op jit(solution)/shard_map/ppermute | solution.py:282
  23.8 2.0 %shard_map.96 = (bf16[256,1024]{1,0:T(8,128)(2,1)}, bf16[256,1024]{1,0:T(8,128)(2,1)}) custom-call(s32[4,8]{1,0:T(4,128)S(4)} %get-tuple-element.50.table, bf16[4096,256]{1,0:T(8,128)(2,1)S(1)} %get-tuple-element.43.probs_ref, bf16[4096,256]{1,0:T(8,128)(2,1)S(1)} %get-tuple-element.51.ds_ref, bf16[1024,256]{1,0:T(8,128)(2,1)S(1)} %get-tuple-element.52.k_pool, ...), custom_call_target="tpu_custom_call" | custom-call | flops 536870912 | bytes 2097152 | tf_op jit(solution)/shard_map/pallas_call | solution.py:200
  25.8 1.3 %collective-permute-done.7 = bf16[256,256]{1,0:T(8,128)(2,1)S(1)} collective-permute-done((bf16[256,256]{1,0:T(8,128)(2,1)S(1)}, bf16[256,256]{1,0:T(8,128)(2,1)S(1)}, u32[]{:S(2)}, u32[]{:S(2)}) %collective-permute-start.7) | collective-permute-done | bytes 131104 | tf_op jit(solution)/shard_map/ppermute | solution.py:282
  27.1 0.0 collective-permute-done.8
  27.1 0.1 collective-permute-done.9
  27.2 0.7 %add_convert_fusion = bf16[256,256]{1,0:T(8,128)(2,1)} fusion(bf16[256,256]{1,0:T(8,128)(2,1)S(1)} %collective-permute-done.8, bf16[256,256]{1,0:T(8,128)(2,1)S(1)} %collective-permute-done.7, f32[256,256]{1,0:T(8,128)S(1)} %get-tuple-element.64, bf16[256,256]{1,0:T(8,128)(2,1)S(1)} %collective-permute-done.6), kind=kLoop, calls=%fused_computation | loop fusion | flops 458752 | bytes 786432 | tf_op jit(solution)/shard_map/convert_element_type | solution.py:295
  27.9 0.4 %collective-permute-done.10 = bf16[256,256]{1,0:T(8,128)(2,1)S(1)} collective-permute-done((bf16[256,256]{1,0:T(8,128)(2,1)S(1)}, bf16[256,256]{1,0:T(8,128)(2,1)S(1)}, u32[]{:S(2)}, u32[]{:S(2)}) %collective-permute-start.10) | collective-permute-done | bytes 131104 | tf_op jit(solution)/shard_map/ppermute | solution.py:282
  28.3 1.0 %collective-permute-done.11 = bf16[256,256]{1,0:T(8,128)(2,1)S(1)} collective-permute-done((bf16[256,256]{1,0:T(8,128)(2,1)S(1)}, bf16[256,256]{1,0:T(8,128)(2,1)S(1)}, u32[]{:S(2)}, u32[]{:S(2)}) %collective-permute-start.11) | collective-permute-done | bytes 131104 | tf_op jit(solution)/shard_map/ppermute | solution.py:282
  29.3 0.7 %add_convert_fusion.1 = bf16[256,256]{1,0:T(8,128)(2,1)} fusion(bf16[256,256]{1,0:T(8,128)(2,1)S(1)} %collective-permute-done.9, bf16[256,256]{1,0:T(8,128)(2,1)S(1)} %collective-permute-done.11, f32[256,256]{1,0:T(8,128)S(1)} %get-tuple-element.60, bf16[256,256]{1,0:T(8,128)(2,1)S(1)} %collective-permute-done.10), kind=kLoop, calls=%fused_computation.1 | loop fusion | flops 458752 | bytes 786432 | tf_op jit(solution)/shard_map/convert_element_type | solution.py:295
Async XLA Ops:
  0.6 9.8 %collective-permute-start = (bf16[256,256]{1,0:T(8,128)(2,1)}, bf16[256,256]{1,0:T(8,128)(2,1)S(1)}, u32[]{:S(2)}, u32[]{:S(2)}) collective-permute-start(bf16[256,256]{1,0:T(8,128)(2,1)} %refs_4_.1), channel_id=1, source_target_pairs={{0,8},{8,0},{16,24},{24,16},{1,17},{9,25},{17,1},{25,9},{2,10},{10... | collective-permute-start | bytes 393224 | tf_op jit(solution)/shard_map/ppermute | solution.py:282
  3.6 7.5 %collective-permute-start.2 = (bf16[256,256]{1,0:T(8,128)(2,1)}, bf16[256,256]{1,0:T(8,128)(2,1)S(1)}, u32[]{:S(2)}, u32[]{:S(2)}) collective-permute-start(bf16[256,256]{1,0:T(8,128)(2,1)} %refs_4_.1), channel_id=1, source_target_pairs={{0,16},{8,24},{16,0},{24,8},{1,9},{9,1},{17,25},{25,17},{2,18},{10... | collective-permute-start | bytes 393224 | tf_op jit(solution)/shard_map/ppermute | solution.py:282
  5.2 7.6 %collective-permute-start.1 = (bf16[256,256]{1,0:T(8,128)(2,1)}, bf16[256,256]{1,0:T(8,128)(2,1)S(1)}, u32[]{:S(2)}, u32[]{:S(2)}) collective-permute-start(bf16[256,256]{1,0:T(8,128)(2,1)} %refs_4_.1), channel_id=1, source_target_pairs={{0,24},{8,16},{16,8},{24,0},{1,25},{9,17},{17,9},{25,1},{2,26},{10... | collective-permute-start | bytes 393224 | tf_op jit(solution)/shard_map/ppermute | solution.py:282
  6.9 9.5 %collective-permute-start.5 = (bf16[256,256]{1,0:T(8,128)(2,1)S(1)}, bf16[256,256]{1,0:T(8,128)(2,1)S(1)}, u32[]{:S(2)}, u32[]{:S(2)}) collective-permute-start(bf16[256,256]{1,0:T(8,128)(2,1)S(1)} %get-tuple-element.45.refs_3_), channel_id=1, source_target_pairs={{0,8},{8,0},{16,24},{24,16},{1,17},{9,25},{17,1},{25,9},{2,10},{10... | collective-permute-start | bytes 393224 | tf_op jit(solution)/shard_map/ppermute | solution.py:282
  8.9 9.2 %collective-permute-start.4 = (bf16[256,256]{1,0:T(8,128)(2,1)S(1)}, bf16[256,256]{1,0:T(8,128)(2,1)S(1)}, u32[]{:S(2)}, u32[]{:S(2)}) collective-permute-start(bf16[256,256]{1,0:T(8,128)(2,1)S(1)} %get-tuple-element.45.refs_3_), channel_id=1, source_target_pairs={{0,16},{8,24},{16,0},{24,8},{1,9},{9,1},{17,25},{25,17},{2,18},{10... | collective-permute-start | bytes 393224 | tf_op jit(solution)/shard_map/ppermute | solution.py:282
  10.4 7.7 %collective-permute-start.3 = (bf16[256,256]{1,0:T(8,128)(2,1)S(1)}, bf16[256,256]{1,0:T(8,128)(2,1)S(1)}, u32[]{:S(2)}, u32[]{:S(2)}) collective-permute-start(bf16[256,256]{1,0:T(8,128)(2,1)S(1)} %get-tuple-element.45.refs_3_), channel_id=1, source_target_pairs={{0,24},{8,16},{16,8},{24,0},{1,25},{9,17},{17,9},{25,1},{2,26},{10... | collective-permute-start | bytes 393224 | tf_op jit(solution)/shard_map/ppermute | solution.py:282
  14.6 7.1 %collective-permute-start.6 = (bf16[256,256]{1,0:T(8,128)(2,1)S(1)}, bf16[256,256]{1,0:T(8,128)(2,1)S(1)}, u32[]{:S(2)}, u32[]{:S(2)}) collective-permute-start(bf16[256,256]{1,0:T(8,128)(2,1)S(1)} %get-tuple-element.48), channel_id=1, source_target_pairs={{0,8},{8,0},{16,24},{24,16},{1,17},{9,25},{17,1},{25,9},{2,10},{10... | collective-permute-start | bytes 393224 | tf_op jit(solution)/shard_map/ppermute | solution.py:282
  15.9 11.2 %collective-permute-start.7 = (bf16[256,256]{1,0:T(8,128)(2,1)S(1)}, bf16[256,256]{1,0:T(8,128)(2,1)S(1)}, u32[]{:S(2)}, u32[]{:S(2)}) collective-permute-start(bf16[256,256]{1,0:T(8,128)(2,1)S(1)} %get-tuple-element.55), channel_id=1, source_target_pairs={{0,16},{8,24},{16,0},{24,8},{1,9},{9,1},{17,25},{25,17},{2,18},{10... | collective-permute-start | bytes 393224 | tf_op jit(solution)/shard_map/ppermute | solution.py:282
  16.4 10.7 %collective-permute-start.8 = (bf16[256,256]{1,0:T(8,128)(2,1)S(1)}, bf16[256,256]{1,0:T(8,128)(2,1)S(1)}, u32[]{:S(2)}, u32[]{:S(2)}) collective-permute-start(bf16[256,256]{1,0:T(8,128)(2,1)S(1)} %get-tuple-element.56), channel_id=1, source_target_pairs={{0,24},{8,16},{16,8},{24,0},{1,25},{9,17},{17,9},{25,1},{2,26},{10... | collective-permute-start | bytes 393224 | tf_op jit(solution)/shard_map/ppermute | solution.py:282
  20.2 7.0 %collective-permute-start.9 = (bf16[256,256]{1,0:T(8,128)(2,1)S(1)}, bf16[256,256]{1,0:T(8,128)(2,1)S(1)}, u32[]{:S(2)}, u32[]{:S(2)}) collective-permute-start(bf16[256,256]{1,0:T(8,128)(2,1)S(1)} %get-tuple-element.57), channel_id=1, source_target_pairs={{0,24},{8,16},{16,8},{24,0},{1,25},{9,17},{17,9},{25,1},{2,26},{10... | collective-permute-start | bytes 393224 | tf_op jit(solution)/shard_map/ppermute | solution.py:282
  21.7 6.6 %collective-permute-start.10 = (bf16[256,256]{1,0:T(8,128)(2,1)S(1)}, bf16[256,256]{1,0:T(8,128)(2,1)S(1)}, u32[]{:S(2)}, u32[]{:S(2)}) collective-permute-start(bf16[256,256]{1,0:T(8,128)(2,1)S(1)} %get-tuple-element.61), channel_id=1, source_target_pairs={{0,8},{8,0},{16,24},{24,16},{1,17},{9,25},{17,1},{25,9},{2,10},{10... | collective-permute-start | bytes 393224 | tf_op jit(solution)/shard_map/ppermute | solution.py:282
  22.8 6.5 %collective-permute-start.11 = (bf16[256,256]{1,0:T(8,128)(2,1)S(1)}, bf16[256,256]{1,0:T(8,128)(2,1)S(1)}, u32[]{:S(2)}, u32[]{:S(2)}) collective-permute-start(bf16[256,256]{1,0:T(8,128)(2,1)S(1)} %get-tuple-element.62), channel_id=1, source_target_pairs={{0,16},{8,24},{16,0},{24,8},{1,9},{9,1},{17,25},{25,17},{2,18},{10... | collective-permute-start | bytes 393224 | tf_op jit(solution)/shard_map/ppermute | solution.py:282

commit v2 on v0

--- a/solution.py
+++ b/solution.py
@@ -190,6 +190,19 @@
         copy.wait()
 
 
+def total_kernel(*refs):
+    *parts, out_any, out_ref, sem = refs
+    copies = []
+    for i in range(0, out_ref.shape[0], BLOCK):
+        rows = pl.ds(i, BLOCK)
+        total = sum(part[rows].astype(jnp.float32) for part in parts)
+        out_ref[rows] = total.astype(out_ref.dtype)
+        copies.append(pltpu.make_async_copy(out_ref.at[rows], out_any.at[rows], sem.at[len(copies)]))
+        copies[-1].start()
+    for copy in copies:
+        copy.wait()
+
+
 SMEM = pl.BlockSpec(memory_space=pltpu.SMEM)
 HBM = pl.BlockSpec(memory_space=pltpu.HBM)
 VMEM = pl.BlockSpec(memory_space=pltpu.VMEM)
@@ -292,7 +305,10 @@
         return sent
 
     def total(grads):
-        return sum(grad.astype(jnp.float32) for grad in grads).astype(jnp.bfloat16)
+        result = (grads[0].shape, jnp.bfloat16)
+        semaphores = pltpu.SemaphoreType.DMA((grads[0].shape[0] // BLOCK,))
+        scratch = [pltpu.VMEM(*result), semaphores]
+        return run_kernel(total_kernel, grads, [], [result], scratch, 0, HBM)[0]
 
     parts = range(1, cycle_size)
     key_parts = [swap(keys, part) for part in parts]

time: 29.8 us -> 29.8 us (level)
  other arithmetic: 1.43 us -> 0 us
  Pallas kernels: 7.65 us -> 9.07 us
    convert_element_type x2 -> x0, other arithmetic: 1.43 us -> none  [total(): sum((grad.astype(jnp.float32) for grad in grads)).astype(jnp.bfloat16)]
    pallas_call x4 -> x6, Pallas kernels: 7.65 us -> 9.07 us  [run_kernel(): pl.pallas_call(kernel, out_shape=[result if hasattr(result, 'memory_space...]
  transfers between devices with their start and end apart: 12 -> 12, of which waited for: 5 -> 5; matrix products, arithmetic and copies ran while one was open for 2% -> 0% of each run, Pallas kernels for 26% -> 28%
where the time goes in v2:
time: 29.8 us; the launch traced here: 29.6 us
  starting transfers between devices  16.8 us (56%)
  Pallas kernels  9.07 us (30%)
  waiting for transfers between devices  3.06 us (10%)
  between operations  0.68 us (2%)
    ppermute x12, starting transfers between devices, swap(): return lax.ppermute(array, ('seq', 'dp'), pairs)  16.8 us
    pallas_call x6, Pallas kernels, run_kernel(): pl.pallas_call(kernel, out_shape=[result if hasattr(result, 'memory_space...  9.07 us
    ppermute x12, waiting for transfers between devices, swap(): return lax.ppermute(array, ('seq', 'dp'), pairs)  3.06 us
  transfers between devices with their start and end apart: 12, of which 5 were waited for; matrix products, arithmetic and copies ran while one was open for 0% of the time, Pallas kernels for 28%

profile of v2, /device:TPU:0, one launch (start us, length us, event | category | flops | bytes accessed | tf_op | source)
XLA Modules:
  0.0 29.6 jit_solution(8178586256345261489)
XLA Ops:
  0.6 4.0 %collective-permute-start = (bf16[256,256]{1,0:T(8,128)(2,1)}, bf16[256,256]{1,0:T(8,128)(2,1)S(1)}, u32[]{:S(2)}, u32[]{:S(2)}) collective-permute-start(bf16[256,256]{1,0:T(8,128)(2,1)} %refs_4_.1), channel_id=1, source_target_pairs={{0,24},{8,16},{16,8},{24,0},{1,25},{9,17},{17,9},{25,1},{2,26},{10... | collective-permute-start | bytes 393224 | tf_op jit(solution)/shard_map/ppermute | solution.py:295
  4.6 0.5 %collective-permute-start.2 = (bf16[256,256]{1,0:T(8,128)(2,1)}, bf16[256,256]{1,0:T(8,128)(2,1)S(1)}, u32[]{:S(2)}, u32[]{:S(2)}) collective-permute-start(bf16[256,256]{1,0:T(8,128)(2,1)} %refs_4_.1), channel_id=1, source_target_pairs={{0,8},{8,0},{16,24},{24,16},{1,17},{9,25},{17,1},{25,9},{2,10},{10... | collective-permute-start | bytes 393224 | tf_op jit(solution)/shard_map/ppermute | solution.py:295
  5.1 0.1 collective-permute-start.1
  5.2 1.7 %shard_map.93 = (s32[4,8]{1,0:T(4,128)S(4)}, bf16[2048,128]{1,0:T(8,128)(2,1)S(1)}, bf16[2048,128]{1,0:T(8,128)(2,1)S(1)}, bf16[1024,256]{1,0:T(8,128)(2,1)S(1)}...) custom-call(s32[3,16]{1,0:T(4,128)} %bitcast.1, ...), custom_call_target="tpu_custom_call" | custom-call | flops 268435456 | bytes 1048576 | tf_op jit(solution)/shard_map/pallas_call | solution.py:213
  7.0 2.0 %collective-permute-start.5 = (bf16[256,256]{1,0:T(8,128)(2,1)S(1)}, bf16[256,256]{1,0:T(8,128)(2,1)S(1)}, u32[]{:S(2)}, u32[]{:S(2)}) collective-permute-start(bf16[256,256]{1,0:T(8,128)(2,1)S(1)} %get-tuple-element.45.refs_3_), channel_id=1, source_target_pairs={{0,8},{8,0},{16,24},{24,16},{1,17},{9,25},{17,1},{25,9},{2,10},{10... | collective-permute-start | bytes 393224 | tf_op jit(solution)/shard_map/ppermute | solution.py:295
  8.9 1.5 %collective-permute-start.4 = (bf16[256,256]{1,0:T(8,128)(2,1)S(1)}, bf16[256,256]{1,0:T(8,128)(2,1)S(1)}, u32[]{:S(2)}, u32[]{:S(2)}) collective-permute-start(bf16[256,256]{1,0:T(8,128)(2,1)S(1)} %get-tuple-element.45.refs_3_), channel_id=1, source_target_pairs={{0,16},{8,24},{16,0},{24,8},{1,9},{9,1},{17,25},{25,17},{2,18},{10... | collective-permute-start | bytes 393224 | tf_op jit(solution)/shard_map/ppermute | solution.py:295
  10.4 0.0 collective-permute-done.refs_0_
  10.4 1.6 %collective-permute-start.3 = (bf16[256,256]{1,0:T(8,128)(2,1)S(1)}, bf16[256,256]{1,0:T(8,128)(2,1)S(1)}, u32[]{:S(2)}, u32[]{:S(2)}) collective-permute-start(bf16[256,256]{1,0:T(8,128)(2,1)S(1)} %get-tuple-element.45.refs_3_), channel_id=1, source_target_pairs={{0,24},{8,16},{16,8},{24,0},{1,25},{9,17},{17,9},{25,1},{2,26},{10... | collective-permute-start | bytes 393224 | tf_op jit(solution)/shard_map/ppermute | solution.py:295
  12.1 0.3 collective-permute-done.2.refs_2_
  12.4 0.0 collective-permute-done.1.refs_1_
  12.4 1.8 %shard_map.94 = (bf16[4096,256]{1,0:T(8,128)(2,1)S(1)}, bf16[1024,256]{1,0:T(8,128)(2,1)S(1)}, f32[1024,256]{1,0:T(8,128)S(1)}, f32[256,256]{1,0:T(8,128)S(1)}, ...) custom-call(s32[4,8]{1,0:T(4,128)S(4)} %get-tuple-element.50.table, ...), custom_call_target="tpu_custom_call", output_to_operand_aliasing={{2}: (3, {})} | custom-call | flops 536870912 | bytes 2097152 | tf_op jit(solution)/shard_map/pallas_call | solution.py:213
  14.2 1.7 %collective-permute-start.6 = (bf16[256,256]{1,0:T(8,128)(2,1)S(1)}, bf16[256,256]{1,0:T(8,128)(2,1)S(1)}, u32[]{:S(2)}, u32[]{:S(2)}) collective-permute-start(bf16[256,256]{1,0:T(8,128)(2,1)S(1)} %get-tuple-element.48), channel_id=1, source_target_pairs={{0,8},{8,0},{16,24},{24,16},{1,17},{9,25},{17,1},{25,9},{2,10},{10... | collective-permute-start | bytes 393224 | tf_op jit(solution)/shard_map/ppermute | solution.py:295
  15.9 0.6 %collective-permute-start.7 = (bf16[256,256]{1,0:T(8,128)(2,1)S(1)}, bf16[256,256]{1,0:T(8,128)(2,1)S(1)}, u32[]{:S(2)}, u32[]{:S(2)}) collective-permute-start(bf16[256,256]{1,0:T(8,128)(2,1)S(1)} %get-tuple-element.55), channel_id=1, source_target_pairs={{0,16},{8,24},{16,0},{24,8},{1,9},{9,1},{17,25},{25,17},{2,18},{10... | collective-permute-start | bytes 393224 | tf_op jit(solution)/shard_map/ppermute | solution.py:295
  16.6 0.0 collective-permute-done.5.refs_2_
  16.6 1.2 %collective-permute-start.8 = (bf16[256,256]{1,0:T(8,128)(2,1)S(1)}, bf16[256,256]{1,0:T(8,128)(2,1)S(1)}, u32[]{:S(2)}, u32[]{:S(2)}) collective-permute-start(bf16[256,256]{1,0:T(8,128)(2,1)S(1)} %get-tuple-element.56), channel_id=1, source_target_pairs={{0,24},{8,16},{16,8},{24,0},{1,25},{9,17},{17,9},{25,1},{2,26},{10... | collective-permute-start | bytes 393224 | tf_op jit(solution)/shard_map/ppermute | solution.py:295
  17.8 0.0 collective-permute-done.4.refs_1_
  17.8 0.0 collective-permute-done.3.refs_0_
  17.8 2.0 %shard_map.95 = (bf16[4096,256]{1,0:T(8,128)(2,1)S(1)}, bf16[1024,256]{1,0:T(8,128)(2,1)S(1)}, f32[1024,256]{1,0:T(8,128)S(1)}, f32[256,256]{1,0:T(8,128)S(1)}, ...) custom-call(s32[4,8]{1,0:T(4,128)S(4)} %get-tuple-element.50.table, ...), custom_call_target="tpu_custom_call", output_to_operand_aliasing={{2}: (4, {})} | custom-call | flops 536870912 | bytes 2097152 | tf_op jit(solution)/shard_map/pallas_call | solution.py:213
  19.9 2.8 %collective-permute-start.9 = (bf16[256,256]{1,0:T(8,128)(2,1)S(1)}, bf16[256,256]{1,0:T(8,128)(2,1)S(1)}, u32[]{:S(2)}, u32[]{:S(2)}) collective-permute-start(bf16[256,256]{1,0:T(8,128)(2,1)S(1)} %get-tuple-element.57), channel_id=1, source_target_pairs={{0,24},{8,16},{16,8},{24,0},{1,25},{9,17},{17,9},{25,1},{2,26},{10... | collective-permute-start | bytes 393224 | tf_op jit(solution)/shard_map/ppermute | solution.py:295
  22.6 0.0 collective-permute-done.6.refs_1_
  22.6 0.0 collective-permute-start.10
  22.6 0.8 %collective-permute-start.11 = (bf16[256,256]{1,0:T(8,128)(2,1)S(1)}, bf16[256,256]{1,0:T(8,128)(2,1)S(1)}, u32[]{:S(2)}, u32[]{:S(2)}) collective-permute-start(bf16[256,256]{1,0:T(8,128)(2,1)S(1)} %get-tuple-element.62), channel_id=1, source_target_pairs={{0,16},{8,24},{16,0},{24,8},{1,9},{9,1},{17,25},{25,17},{2,18},{10... | collective-permute-start | bytes 393224 | tf_op jit(solution)/shard_map/ppermute | solution.py:295
  23.4 2.0 %shard_map.96 = (bf16[256,1024]{1,0:T(8,128)(2,1)}, bf16[256,1024]{1,0:T(8,128)(2,1)}) custom-call(s32[4,8]{1,0:T(4,128)S(4)} %get-tuple-element.50.table, bf16[4096,256]{1,0:T(8,128)(2,1)S(1)} %get-tuple-element.43.probs_ref, bf16[4096,256]{1,0:T(8,128)(2,1)S(1)} %get-tuple-element.51.ds_ref, bf16[1024,256]{1,0:T(8,128)(2,1)S(1)} %get-tuple-element.52.k_pool, ...), custom_call_target="tpu_custom_call" | custom-call | flops 536870912 | bytes 2097152 | tf_op jit(solution)/shard_map/pallas_call | solution.py:213
  25.5 1.0 %collective-permute-done.7.refs_2_ = bf16[256,256]{1,0:T(8,128)(2,1)S(1)} collective-permute-done((bf16[256,256]{1,0:T(8,128)(2,1)S(1)}, bf16[256,256]{1,0:T(8,128)(2,1)S(1)}, u32[]{:S(2)}, u32[]{:S(2)}) %collective-permute-start.7) | collective-permute-done | bytes 131104 | tf_op jit(solution)/shard_map/ppermute | solution.py:295
  26.4 0.0 collective-permute-done.8.refs_3_
  26.4 0.4 %collective-permute-done.9.refs_3_ = bf16[256,256]{1,0:T(8,128)(2,1)S(1)} collective-permute-done((bf16[256,256]{1,0:T(8,128)(2,1)S(1)}, bf16[256,256]{1,0:T(8,128)(2,1)S(1)}, u32[]{:S(2)}, u32[]{:S(2)}) %collective-permute-start.9) | collective-permute-done | bytes 131104 | tf_op jit(solution)/shard_map/ppermute | solution.py:295
  26.9 0.7 %shard_map.98 = bf16[256,256]{1,0:T(8,128)(2,1)} custom-call(f32[256,256]{1,0:T(8,128)S(1)} %get-tuple-element.64.refs_0_, bf16[256,256]{1,0:T(8,128)(2,1)S(1)} %collective-permute-done.6.refs_1_, bf16[256,256]{1,0:T(8,128)(2,1)S(1)} %collective-permute-done.7.refs_2_, bf16[256,256]{1,0:T(8,128)(2,1)S(1)} %collective-permute-done.8.refs_3_), custom_call_target="tpu_custom_call" | custom-call | tf_op jit(solution)/shard_map/pallas_call | solution.py:213
  27.6 0.8 %collective-permute-done.10.refs_1_ = bf16[256,256]{1,0:T(8,128)(2,1)S(1)} collective-permute-done((bf16[256,256]{1,0:T(8,128)(2,1)S(1)}, bf16[256,256]{1,0:T(8,128)(2,1)S(1)}, u32[]{:S(2)}, u32[]{:S(2)}) %collective-permute-start.10) | collective-permute-done | bytes 131104 | tf_op jit(solution)/shard_map/ppermute | solution.py:295
  28.4 0.6 %collective-permute-done.11.refs_2_ = bf16[256,256]{1,0:T(8,128)(2,1)S(1)} collective-permute-done((bf16[256,256]{1,0:T(8,128)(2,1)S(1)}, bf16[256,256]{1,0:T(8,128)(2,1)S(1)}, u32[]{:S(2)}, u32[]{:S(2)}) %collective-permute-start.11) | collective-permute-done | bytes 131104 | tf_op jit(solution)/shard_map/ppermute | solution.py:295
  28.9 0.7 %shard_map.97 = bf16[256,256]{1,0:T(8,128)(2,1)} custom-call(f32[256,256]{1,0:T(8,128)S(1)} %get-tuple-element.60.refs_0_, bf16[256,256]{1,0:T(8,128)(2,1)S(1)} %collective-permute-done.10.refs_1_, bf16[256,256]{1,0:T(8,128)(2,1)S(1)} %collective-permute-done.11.refs_2_, bf16[256,256]{1,0:T(8,128)(2,1)S(1)} %collective-permute-done.9.refs_3_), custom_call_target="tpu_custom_call" | custom-call | tf_op jit(solution)/shard_map/pallas_call | solution.py:213
Async XLA Ops:
  0.6 9.8 %collective-permute-start = (bf16[256,256]{1,0:T(8,128)(2,1)}, bf16[256,256]{1,0:T(8,128)(2,1)S(1)}, u32[]{:S(2)}, u32[]{:S(2)}) collective-permute-start(bf16[256,256]{1,0:T(8,128)(2,1)} %refs_4_.1), channel_id=1, source_target_pairs={{0,24},{8,16},{16,8},{24,0},{1,25},{9,17},{17,9},{25,1},{2,26},{10... | collective-permute-start | bytes 393224 | tf_op jit(solution)/shard_map/ppermute | solution.py:295
  4.6 7.8 %collective-permute-start.2 = (bf16[256,256]{1,0:T(8,128)(2,1)}, bf16[256,256]{1,0:T(8,128)(2,1)S(1)}, u32[]{:S(2)}, u32[]{:S(2)}) collective-permute-start(bf16[256,256]{1,0:T(8,128)(2,1)} %refs_4_.1), channel_id=1, source_target_pairs={{0,8},{8,0},{16,24},{24,16},{1,17},{9,25},{17,1},{25,9},{2,10},{10... | collective-permute-start | bytes 393224 | tf_op jit(solution)/shard_map/ppermute | solution.py:295
  5.1 7.3 %collective-permute-start.1 = (bf16[256,256]{1,0:T(8,128)(2,1)}, bf16[256,256]{1,0:T(8,128)(2,1)S(1)}, u32[]{:S(2)}, u32[]{:S(2)}) collective-permute-start(bf16[256,256]{1,0:T(8,128)(2,1)} %refs_4_.1), channel_id=1, source_target_pairs={{0,16},{8,24},{16,0},{24,8},{1,9},{9,1},{17,25},{25,17},{2,18},{10... | collective-permute-start | bytes 393224 | tf_op jit(solution)/shard_map/ppermute | solution.py:295
  7.0 9.6 %collective-permute-start.5 = (bf16[256,256]{1,0:T(8,128)(2,1)S(1)}, bf16[256,256]{1,0:T(8,128)(2,1)S(1)}, u32[]{:S(2)}, u32[]{:S(2)}) collective-permute-start(bf16[256,256]{1,0:T(8,128)(2,1)S(1)} %get-tuple-element.45.refs_3_), channel_id=1, source_target_pairs={{0,8},{8,0},{16,24},{24,16},{1,17},{9,25},{17,1},{25,9},{2,10},{10... | collective-permute-start | bytes 393224 | tf_op jit(solution)/shard_map/ppermute | solution.py:295
  8.9 8.9 %collective-permute-start.4 = (bf16[256,256]{1,0:T(8,128)(2,1)S(1)}, bf16[256,256]{1,0:T(8,128)(2,1)S(1)}, u32[]{:S(2)}, u32[]{:S(2)}) collective-permute-start(bf16[256,256]{1,0:T(8,128)(2,1)S(1)} %get-tuple-element.45.refs_3_), channel_id=1, source_target_pairs={{0,16},{8,24},{16,0},{24,8},{1,9},{9,1},{17,25},{25,17},{2,18},{10... | collective-permute-start | bytes 393224 | tf_op jit(solution)/shard_map/ppermute | solution.py:295
  10.4 7.4 %collective-permute-start.3 = (bf16[256,256]{1,0:T(8,128)(2,1)S(1)}, bf16[256,256]{1,0:T(8,128)(2,1)S(1)}, u32[]{:S(2)}, u32[]{:S(2)}) collective-permute-start(bf16[256,256]{1,0:T(8,128)(2,1)S(1)} %get-tuple-element.45.refs_3_), channel_id=1, source_target_pairs={{0,24},{8,16},{16,8},{24,0},{1,25},{9,17},{17,9},{25,1},{2,26},{10... | collective-permute-start | bytes 393224 | tf_op jit(solution)/shard_map/ppermute | solution.py:295
  14.2 8.4 %collective-permute-start.6 = (bf16[256,256]{1,0:T(8,128)(2,1)S(1)}, bf16[256,256]{1,0:T(8,128)(2,1)S(1)}, u32[]{:S(2)}, u32[]{:S(2)}) collective-permute-start(bf16[256,256]{1,0:T(8,128)(2,1)S(1)} %get-tuple-element.48), channel_id=1, source_target_pairs={{0,8},{8,0},{16,24},{24,16},{1,17},{9,25},{17,1},{25,9},{2,10},{10... | collective-permute-start | bytes 393224 | tf_op jit(solution)/shard_map/ppermute | solution.py:295
  15.9 10.5 %collective-permute-start.7 = (bf16[256,256]{1,0:T(8,128)(2,1)S(1)}, bf16[256,256]{1,0:T(8,128)(2,1)S(1)}, u32[]{:S(2)}, u32[]{:S(2)}) collective-permute-start(bf16[256,256]{1,0:T(8,128)(2,1)S(1)} %get-tuple-element.55), channel_id=1, source_target_pairs={{0,16},{8,24},{16,0},{24,8},{1,9},{9,1},{17,25},{25,17},{2,18},{10... | collective-permute-start | bytes 393224 | tf_op jit(solution)/shard_map/ppermute | solution.py:295
  16.6 9.9 %collective-permute-start.8 = (bf16[256,256]{1,0:T(8,128)(2,1)S(1)}, bf16[256,256]{1,0:T(8,128)(2,1)S(1)}, u32[]{:S(2)}, u32[]{:S(2)}) collective-permute-start(bf16[256,256]{1,0:T(8,128)(2,1)S(1)} %get-tuple-element.56), channel_id=1, source_target_pairs={{0,24},{8,16},{16,8},{24,0},{1,25},{9,17},{17,9},{25,1},{2,26},{10... | collective-permute-start | bytes 393224 | tf_op jit(solution)/shard_map/ppermute | solution.py:295
  19.9 7.0 %collective-permute-start.9 = (bf16[256,256]{1,0:T(8,128)(2,1)S(1)}, bf16[256,256]{1,0:T(8,128)(2,1)S(1)}, u32[]{:S(2)}, u32[]{:S(2)}) collective-permute-start(bf16[256,256]{1,0:T(8,128)(2,1)S(1)} %get-tuple-element.57), channel_id=1, source_target_pairs={{0,24},{8,16},{16,8},{24,0},{1,25},{9,17},{17,9},{25,1},{2,26},{10... | collective-permute-start | bytes 393224 | tf_op jit(solution)/shard_map/ppermute | solution.py:295
  22.6 5.7 %collective-permute-start.10 = (bf16[256,256]{1,0:T(8,128)(2,1)S(1)}, bf16[256,256]{1,0:T(8,128)(2,1)S(1)}, u32[]{:S(2)}, u32[]{:S(2)}) collective-permute-start(bf16[256,256]{1,0:T(8,128)(2,1)S(1)} %get-tuple-element.61), channel_id=1, source_target_pairs={{0,8},{8,0},{16,24},{24,16},{1,17},{9,25},{17,1},{25,9},{2,10},{10... | collective-permute-start | bytes 393224 | tf_op jit(solution)/shard_map/ppermute | solution.py:295
  22.6 6.3 %collective-permute-start.11 = (bf16[256,256]{1,0:T(8,128)(2,1)S(1)}, bf16[256,256]{1,0:T(8,128)(2,1)S(1)}, u32[]{:S(2)}, u32[]{:S(2)}) collective-permute-start(bf16[256,256]{1,0:T(8,128)(2,1)S(1)} %get-tuple-element.62), channel_id=1, source_target_pairs={{0,16},{8,24},{16,0},{24,8},{1,9},{9,1},{17,25},{25,17},{2,18},{10... | collective-permute-start | bytes 393224 | tf_op jit(solution)/shard_map/ppermute | solution.py:295

commit v3 on v2

--- a/solution.py
+++ b/solution.py
@@ -23,7 +23,7 @@
 dot = functools.partial(lax.dot_general, preferred_element_type=jnp.float32)
 
 KEYS = ENTRIES * BLOCK
-CHUNK = 128
+CHUNK = 64
 FACTOR = SCALE * LOG2E
 ROWS = GROUP * BLOCK
 

time: 29.8 us -> 29.9 us (level)
  no operation moved by 1% of the time
where the time goes in v3:
time: 29.9 us; the launch traced here: 29.7 us
  starting transfers between devices  16.8 us (56%)
  Pallas kernels  9.14 us (31%)
  waiting for transfers between devices  3.05 us (10%)
  between operations  0.68 us (2%)
    ppermute x12, starting transfers between devices, swap(): return lax.ppermute(array, ('seq', 'dp'), pairs)  16.8 us
    pallas_call x6, Pallas kernels, run_kernel(): pl.pallas_call(kernel, out_shape=[result if hasattr(result, 'memory_space...  9.14 us
    ppermute x12, waiting for transfers between devices, swap(): return lax.ppermute(array, ('seq', 'dp'), pairs)  3.05 us
  transfers between devices with their start and end apart: 12, of which 5 were waited for; matrix products, arithmetic and copies ran while one was open for 0% of the time, Pallas kernels for 28%

profile of v3, /device:TPU:0, one launch (start us, length us, event | category | flops | bytes accessed | tf_op | source)
XLA Modules:
  0.0 29.7 jit_solution(16502436389236017736)
XLA Ops:
  0.6 4.0 %collective-permute-start = (bf16[256,256]{1,0:T(8,128)(2,1)}, bf16[256,256]{1,0:T(8,128)(2,1)S(1)}, u32[]{:S(2)}, u32[]{:S(2)}) collective-permute-start(bf16[256,256]{1,0:T(8,128)(2,1)} %refs_4_.1), channel_id=1, source_target_pairs={{0,24},{8,16},{16,8},{24,0},{1,25},{9,17},{17,9},{25,1},{2,26},{10... | collective-permute-start | bytes 393224 | tf_op jit(solution)/shard_map/ppermute | solution.py:295
  4.6 0.5 %collective-permute-start.2 = (bf16[256,256]{1,0:T(8,128)(2,1)}, bf16[256,256]{1,0:T(8,128)(2,1)S(1)}, u32[]{:S(2)}, u32[]{:S(2)}) collective-permute-start(bf16[256,256]{1,0:T(8,128)(2,1)} %refs_4_.1), channel_id=1, source_target_pairs={{0,8},{8,0},{16,24},{24,16},{1,17},{9,25},{17,1},{25,9},{2,10},{10... | collective-permute-start | bytes 393224 | tf_op jit(solution)/shard_map/ppermute | solution.py:295
  5.1 0.1 collective-permute-start.1
  5.2 1.7 %shard_map.93 = (s32[4,8]{1,0:T(4,128)S(4)}, bf16[2048,128]{1,0:T(8,128)(2,1)S(1)}, bf16[2048,128]{1,0:T(8,128)(2,1)S(1)}, bf16[1024,256]{1,0:T(8,128)(2,1)S(1)}...) custom-call(s32[3,16]{1,0:T(4,128)} %bitcast.1, ...), custom_call_target="tpu_custom_call" | custom-call | flops 268435456 | bytes 1048576 | tf_op jit(solution)/shard_map/pallas_call | solution.py:213
  7.0 2.0 %collective-permute-start.5 = (bf16[256,256]{1,0:T(8,128)(2,1)S(1)}, bf16[256,256]{1,0:T(8,128)(2,1)S(1)}, u32[]{:S(2)}, u32[]{:S(2)}) collective-permute-start(bf16[256,256]{1,0:T(8,128)(2,1)S(1)} %get-tuple-element.45.refs_3_), channel_id=1, source_target_pairs={{0,8},{8,0},{16,24},{24,16},{1,17},{9,25},{17,1},{25,9},{2,10},{10... | collective-permute-start | bytes 393224 | tf_op jit(solution)/shard_map/ppermute | solution.py:295
  8.9 1.5 %collective-permute-start.4 = (bf16[256,256]{1,0:T(8,128)(2,1)S(1)}, bf16[256,256]{1,0:T(8,128)(2,1)S(1)}, u32[]{:S(2)}, u32[]{:S(2)}) collective-permute-start(bf16[256,256]{1,0:T(8,128)(2,1)S(1)} %get-tuple-element.45.refs_3_), channel_id=1, source_target_pairs={{0,16},{8,24},{16,0},{24,8},{1,9},{9,1},{17,25},{25,17},{2,18},{10... | collective-permute-start | bytes 393224 | tf_op jit(solution)/shard_map/ppermute | solution.py:295
  10.4 0.0 collective-permute-done.refs_0_
  10.4 1.6 %collective-permute-start.3 = (bf16[256,256]{1,0:T(8,128)(2,1)S(1)}, bf16[256,256]{1,0:T(8,128)(2,1)S(1)}, u32[]{:S(2)}, u32[]{:S(2)}) collective-permute-start(bf16[256,256]{1,0:T(8,128)(2,1)S(1)} %get-tuple-element.45.refs_3_), channel_id=1, source_target_pairs={{0,24},{8,16},{16,8},{24,0},{1,25},{9,17},{17,9},{25,1},{2,26},{10... | collective-permute-start | bytes 393224 | tf_op jit(solution)/shard_map/ppermute | solution.py:295
  12.1 0.3 collective-permute-done.2.refs_2_
  12.4 0.0 collective-permute-done.1.refs_1_
  12.4 1.9 %shard_map.94 = (bf16[4096,256]{1,0:T(8,128)(2,1)S(1)}, bf16[1024,256]{1,0:T(8,128)(2,1)S(1)}, f32[1024,256]{1,0:T(8,128)S(1)}, f32[256,256]{1,0:T(8,128)S(1)}, ...) custom-call(s32[4,8]{1,0:T(4,128)S(4)} %get-tuple-element.50.table, ...), custom_call_target="tpu_custom_call", output_to_operand_aliasing={{2}: (3, {})} | custom-call | flops 536870912 | bytes 2097152 | tf_op jit(solution)/shard_map/pallas_call | solution.py:213
  14.3 1.7 %collective-permute-start.6 = (bf16[256,256]{1,0:T(8,128)(2,1)S(1)}, bf16[256,256]{1,0:T(8,128)(2,1)S(1)}, u32[]{:S(2)}, u32[]{:S(2)}) collective-permute-start(bf16[256,256]{1,0:T(8,128)(2,1)S(1)} %get-tuple-element.48), channel_id=1, source_target_pairs={{0,8},{8,0},{16,24},{24,16},{1,17},{9,25},{17,1},{25,9},{2,10},{10... | collective-permute-start | bytes 393224 | tf_op jit(solution)/shard_map/ppermute | solution.py:295
  16.0 0.6 %collective-permute-start.7 = (bf16[256,256]{1,0:T(8,128)(2,1)S(1)}, bf16[256,256]{1,0:T(8,128)(2,1)S(1)}, u32[]{:S(2)}, u32[]{:S(2)}) collective-permute-start(bf16[256,256]{1,0:T(8,128)(2,1)S(1)} %get-tuple-element.55), channel_id=1, source_target_pairs={{0,16},{8,24},{16,0},{24,8},{1,9},{9,1},{17,25},{25,17},{2,18},{10... | collective-permute-start | bytes 393224 | tf_op jit(solution)/shard_map/ppermute | solution.py:295
  16.6 0.0 collective-permute-done.5.refs_2_
  16.6 1.2 %collective-permute-start.8 = (bf16[256,256]{1,0:T(8,128)(2,1)S(1)}, bf16[256,256]{1,0:T(8,128)(2,1)S(1)}, u32[]{:S(2)}, u32[]{:S(2)}) collective-permute-start(bf16[256,256]{1,0:T(8,128)(2,1)S(1)} %get-tuple-element.56), channel_id=1, source_target_pairs={{0,24},{8,16},{16,8},{24,0},{1,25},{9,17},{17,9},{25,1},{2,26},{10... | collective-permute-start | bytes 393224 | tf_op jit(solution)/shard_map/ppermute | solution.py:295
  17.9 0.0 collective-permute-done.4.refs_1_
  17.9 0.0 collective-permute-done.3.refs_0_
  17.9 2.0 %shard_map.95 = (bf16[4096,256]{1,0:T(8,128)(2,1)S(1)}, bf16[1024,256]{1,0:T(8,128)(2,1)S(1)}, f32[1024,256]{1,0:T(8,128)S(1)}, f32[256,256]{1,0:T(8,128)S(1)}, ...) custom-call(s32[4,8]{1,0:T(4,128)S(4)} %get-tuple-element.50.table, ...), custom_call_target="tpu_custom_call", output_to_operand_aliasing={{2}: (4, {})} | custom-call | flops 536870912 | bytes 2097152 | tf_op jit(solution)/shard_map/pallas_call | solution.py:213
  19.9 2.6 %collective-permute-start.9 = (bf16[256,256]{1,0:T(8,128)(2,1)S(1)}, bf16[256,256]{1,0:T(8,128)(2,1)S(1)}, u32[]{:S(2)}, u32[]{:S(2)}) collective-permute-start(bf16[256,256]{1,0:T(8,128)(2,1)S(1)} %get-tuple-element.57), channel_id=1, source_target_pairs={{0,24},{8,16},{16,8},{24,0},{1,25},{9,17},{17,9},{25,1},{2,26},{10... | collective-permute-start | bytes 393224 | tf_op jit(solution)/shard_map/ppermute | solution.py:295
  22.5 0.0 collective-permute-done.6.refs_1_
  22.5 0.0 collective-permute-start.10
  22.5 0.9 %collective-permute-start.11 = (bf16[256,256]{1,0:T(8,128)(2,1)S(1)}, bf16[256,256]{1,0:T(8,128)(2,1)S(1)}, u32[]{:S(2)}, u32[]{:S(2)}) collective-permute-start(bf16[256,256]{1,0:T(8,128)(2,1)S(1)} %get-tuple-element.62), channel_id=1, source_target_pairs={{0,16},{8,24},{16,0},{24,8},{1,9},{9,1},{17,25},{25,17},{2,18},{10... | collective-permute-start | bytes 393224 | tf_op jit(solution)/shard_map/ppermute | solution.py:295
  23.5 2.0 %shard_map.96 = (bf16[256,1024]{1,0:T(8,128)(2,1)}, bf16[256,1024]{1,0:T(8,128)(2,1)}) custom-call(s32[4,8]{1,0:T(4,128)S(4)} %get-tuple-element.50.table, bf16[4096,256]{1,0:T(8,128)(2,1)S(1)} %get-tuple-element.43.probs_ref, bf16[4096,256]{1,0:T(8,128)(2,1)S(1)} %get-tuple-element.51.ds_ref, bf16[1024,256]{1,0:T(8,128)(2,1)S(1)} %get-tuple-element.52.k_pool, ...), custom_call_target="tpu_custom_call" | custom-call | flops 536870912 | bytes 2097152 | tf_op jit(solution)/shard_map/pallas_call | solution.py:213
  25.5 1.1 %collective-permute-done.7.refs_2_ = bf16[256,256]{1,0:T(8,128)(2,1)S(1)} collective-permute-done((bf16[256,256]{1,0:T(8,128)(2,1)S(1)}, bf16[256,256]{1,0:T(8,128)(2,1)S(1)}, u32[]{:S(2)}, u32[]{:S(2)}) %collective-permute-start.7) | collective-permute-done | bytes 131104 | tf_op jit(solution)/shard_map/ppermute | solution.py:295
  26.6 0.0 collective-permute-done.8.refs_3_
  26.6 0.3 collective-permute-done.9.refs_3_
  26.9 0.7 %shard_map.98 = bf16[256,256]{1,0:T(8,128)(2,1)} custom-call(f32[256,256]{1,0:T(8,128)S(1)} %get-tuple-element.64.refs_0_, bf16[256,256]{1,0:T(8,128)(2,1)S(1)} %collective-permute-done.6.refs_1_, bf16[256,256]{1,0:T(8,128)(2,1)S(1)} %collective-permute-done.7.refs_2_, bf16[256,256]{1,0:T(8,128)(2,1)S(1)} %collective-permute-done.8.refs_3_), custom_call_target="tpu_custom_call" | custom-call | tf_op jit(solution)/shard_map/pallas_call | solution.py:213
  27.6 0.8 %collective-permute-done.10.refs_1_ = bf16[256,256]{1,0:T(8,128)(2,1)S(1)} collective-permute-done((bf16[256,256]{1,0:T(8,128)(2,1)S(1)}, bf16[256,256]{1,0:T(8,128)(2,1)S(1)}, u32[]{:S(2)}, u32[]{:S(2)}) %collective-permute-start.10) | collective-permute-done | bytes 131104 | tf_op jit(solution)/shard_map/ppermute | solution.py:295
  28.4 0.6 %collective-permute-done.11.refs_2_ = bf16[256,256]{1,0:T(8,128)(2,1)S(1)} collective-permute-done((bf16[256,256]{1,0:T(8,128)(2,1)S(1)}, bf16[256,256]{1,0:T(8,128)(2,1)S(1)}, u32[]{:S(2)}, u32[]{:S(2)}) %collective-permute-start.11) | collective-permute-done | bytes 131104 | tf_op jit(solution)/shard_map/ppermute | solution.py:295
  29.0 0.7 %shard_map.97 = bf16[256,256]{1,0:T(8,128)(2,1)} custom-call(f32[256,256]{1,0:T(8,128)S(1)} %get-tuple-element.60.refs_0_, bf16[256,256]{1,0:T(8,128)(2,1)S(1)} %collective-permute-done.10.refs_1_, bf16[256,256]{1,0:T(8,128)(2,1)S(1)} %collective-permute-done.11.refs_2_, bf16[256,256]{1,0:T(8,128)(2,1)S(1)} %collective-permute-done.9.refs_3_), custom_call_target="tpu_custom_call" | custom-call | tf_op jit(solution)/shard_map/pallas_call | solution.py:213
Async XLA Ops:
  0.6 9.8 %collective-permute-start = (bf16[256,256]{1,0:T(8,128)(2,1)}, bf16[256,256]{1,0:T(8,128)(2,1)S(1)}, u32[]{:S(2)}, u32[]{:S(2)}) collective-permute-start(bf16[256,256]{1,0:T(8,128)(2,1)} %refs_4_.1), channel_id=1, source_target_pairs={{0,24},{8,16},{16,8},{24,0},{1,25},{9,17},{17,9},{25,1},{2,26},{10... | collective-permute-start | bytes 393224 | tf_op jit(solution)/shard_map/ppermute | solution.py:295
  4.6 7.8 %collective-permute-start.2 = (bf16[256,256]{1,0:T(8,128)(2,1)}, bf16[256,256]{1,0:T(8,128)(2,1)S(1)}, u32[]{:S(2)}, u32[]{:S(2)}) collective-permute-start(bf16[256,256]{1,0:T(8,128)(2,1)} %refs_4_.1), channel_id=1, source_target_pairs={{0,8},{8,0},{16,24},{24,16},{1,17},{9,25},{17,1},{25,9},{2,10},{10... | collective-permute-start | bytes 393224 | tf_op jit(solution)/shard_map/ppermute | solution.py:295
  5.1 7.3 %collective-permute-start.1 = (bf16[256,256]{1,0:T(8,128)(2,1)}, bf16[256,256]{1,0:T(8,128)(2,1)S(1)}, u32[]{:S(2)}, u32[]{:S(2)}) collective-permute-start(bf16[256,256]{1,0:T(8,128)(2,1)} %refs_4_.1), channel_id=1, source_target_pairs={{0,16},{8,24},{16,0},{24,8},{1,9},{9,1},{17,25},{25,17},{2,18},{10... | collective-permute-start | bytes 393224 | tf_op jit(solution)/shard_map/ppermute | solution.py:295
  7.0 9.7 %collective-permute-start.5 = (bf16[256,256]{1,0:T(8,128)(2,1)S(1)}, bf16[256,256]{1,0:T(8,128)(2,1)S(1)}, u32[]{:S(2)}, u32[]{:S(2)}) collective-permute-start(bf16[256,256]{1,0:T(8,128)(2,1)S(1)} %get-tuple-element.45.refs_3_), channel_id=1, source_target_pairs={{0,8},{8,0},{16,24},{24,16},{1,17},{9,25},{17,1},{25,9},{2,10},{10... | collective-permute-start | bytes 393224 | tf_op jit(solution)/shard_map/ppermute | solution.py:295
  8.9 9.0 %collective-permute-start.4 = (bf16[256,256]{1,0:T(8,128)(2,1)S(1)}, bf16[256,256]{1,0:T(8,128)(2,1)S(1)}, u32[]{:S(2)}, u32[]{:S(2)}) collective-permute-start(bf16[256,256]{1,0:T(8,128)(2,1)S(1)} %get-tuple-element.45.refs_3_), channel_id=1, source_target_pairs={{0,16},{8,24},{16,0},{24,8},{1,9},{9,1},{17,25},{25,17},{2,18},{10... | collective-permute-start | bytes 393224 | tf_op jit(solution)/shard_map/ppermute | solution.py:295
  10.4 7.4 %collective-permute-start.3 = (bf16[256,256]{1,0:T(8,128)(2,1)S(1)}, bf16[256,256]{1,0:T(8,128)(2,1)S(1)}, u32[]{:S(2)}, u32[]{:S(2)}) collective-permute-start(bf16[256,256]{1,0:T(8,128)(2,1)S(1)} %get-tuple-element.45.refs_3_), channel_id=1, source_target_pairs={{0,24},{8,16},{16,8},{24,0},{1,25},{9,17},{17,9},{25,1},{2,26},{10... | collective-permute-start | bytes 393224 | tf_op jit(solution)/shard_map/ppermute | solution.py:295
  14.3 8.2 %collective-permute-start.6 = (bf16[256,256]{1,0:T(8,128)(2,1)S(1)}, bf16[256,256]{1,0:T(8,128)(2,1)S(1)}, u32[]{:S(2)}, u32[]{:S(2)}) collective-permute-start(bf16[256,256]{1,0:T(8,128)(2,1)S(1)} %get-tuple-element.48), channel_id=1, source_target_pairs={{0,8},{8,0},{16,24},{24,16},{1,17},{9,25},{17,1},{25,9},{2,10},{10... | collective-permute-start | bytes 393224 | tf_op jit(solution)/shard_map/ppermute | solution.py:295
  16.0 10.6 %collective-permute-start.7 = (bf16[256,256]{1,0:T(8,128)(2,1)S(1)}, bf16[256,256]{1,0:T(8,128)(2,1)S(1)}, u32[]{:S(2)}, u32[]{:S(2)}) collective-permute-start(bf16[256,256]{1,0:T(8,128)(2,1)S(1)} %get-tuple-element.55), channel_id=1, source_target_pairs={{0,16},{8,24},{16,0},{24,8},{1,9},{9,1},{17,25},{25,17},{2,18},{10... | collective-permute-start | bytes 393224 | tf_op jit(solution)/shard_map/ppermute | solution.py:295
  16.6 10.0 %collective-permute-start.8 = (bf16[256,256]{1,0:T(8,128)(2,1)S(1)}, bf16[256,256]{1,0:T(8,128)(2,1)S(1)}, u32[]{:S(2)}, u32[]{:S(2)}) collective-permute-start(bf16[256,256]{1,0:T(8,128)(2,1)S(1)} %get-tuple-element.56), channel_id=1, source_target_pairs={{0,24},{8,16},{16,8},{24,0},{1,25},{9,17},{17,9},{25,1},{2,26},{10... | collective-permute-start | bytes 393224 | tf_op jit(solution)/shard_map/ppermute | solution.py:295
  19.9 6.9 %collective-permute-start.9 = (bf16[256,256]{1,0:T(8,128)(2,1)S(1)}, bf16[256,256]{1,0:T(8,128)(2,1)S(1)}, u32[]{:S(2)}, u32[]{:S(2)}) collective-permute-start(bf16[256,256]{1,0:T(8,128)(2,1)S(1)} %get-tuple-element.57), channel_id=1, source_target_pairs={{0,24},{8,16},{16,8},{24,0},{1,25},{9,17},{17,9},{25,1},{2,26},{10... | collective-permute-start | bytes 393224 | tf_op jit(solution)/shard_map/ppermute | solution.py:295
  22.5 5.9 %collective-permute-start.10 = (bf16[256,256]{1,0:T(8,128)(2,1)S(1)}, bf16[256,256]{1,0:T(8,128)(2,1)S(1)}, u32[]{:S(2)}, u32[]{:S(2)}) collective-permute-start(bf16[256,256]{1,0:T(8,128)(2,1)S(1)} %get-tuple-element.61), channel_id=1, source_target_pairs={{0,8},{8,0},{16,24},{24,16},{1,17},{9,25},{17,1},{25,9},{2,10},{10... | collective-permute-start | bytes 393224 | tf_op jit(solution)/shard_map/ppermute | solution.py:295
  22.5 6.5 %collective-permute-start.11 = (bf16[256,256]{1,0:T(8,128)(2,1)S(1)}, bf16[256,256]{1,0:T(8,128)(2,1)S(1)}, u32[]{:S(2)}, u32[]{:S(2)}) collective-permute-start(bf16[256,256]{1,0:T(8,128)(2,1)S(1)} %get-tuple-element.62), channel_id=1, source_target_pairs={{0,16},{8,24},{16,0},{24,8},{1,9},{9,1},{17,25},{25,17},{2,18},{10... | collective-permute-start | bytes 393224 | tf_op jit(solution)/shard_map/ppermute | solution.py:295
